TPU v7x, 32 devices: a whole 2x2x4 slice. The times are simulated.
32 devices in a mesh: section: 4 (over y, x), dp: 4 (over z), mp: 2 (over core).
Axes of the slice: x: 2, y: 2, z: 4, core: 2. Of those that a mesh axis runs over, the one named last changes fastest.
Arguments:
- inputs: bfloat16 [8, 256, 1536], P('dp', 'mp'), may hold values from -6 to 6
- cotangent: bfloat16 [8, 256, 1536], P('dp', 'mp'), may hold values from -6 to 6
- width_index: int32 [8], P('dp'), may hold values from 0 to 3, as said below
- qkv_weight: bfloat16 [3, 3072, 1536], P(None, 'section', 'mp'), may hold values from -0.15625 to 0.15625
- out_weight: bfloat16 [3072, 1536], P('section', 'mp'), may hold values from -1.75 to 1.75
- attn_gain: bfloat16 [3072], P('section'), may hold values from 0.5 to 1.5
- ffn_gain: bfloat16 [3072], P('section'), may hold values from 0.5 to 1.5
- up_weight: bfloat16 [3072, 6144], P('section', 'mp'), may hold values from -0.15625 to 0.15625
- down_weight: bfloat16 [3072, 6144], P('section', 'mp'), may hold values from -0.15625 to 0.15625
Outputs:
- layer_out: bfloat16 [4, 8, 256, 1536], P('section', 'dp', 'mp')
- input_grad: bfloat16 [4, 8, 256, 1536], P('section', 'dp', 'mp')
- qkv_grad: float32 [3, 3072, 1536], P(None, ('section', 'dp'), 'mp')
- out_weight_grad: float32 [3072, 1536], P(('section', 'dp'), 'mp')
- attn_gain_grad: float32 [3072], P(('section', 'dp', 'mp'))
- ffn_gain_grad: float32 [3072], P(('section', 'dp', 'mp'))
- up_grad: float32 [3072, 6144], P(('section', 'dp'), 'mp')
- down_grad: float32 [3072, 6144], P(('section', 'dp'), 'mp')
Inputs may be any that keep to these rules, and one draw needn't show every extreme that they name: `width_index`: in each aligned pair of sequences (2i and 2i+1) the two width indices add up to 3.
All inputs are finite; a program needn't handle non-finite values.
Results may differ from a plain program's by a relative error of at most 0.03.
Values may be sent and summed in bfloat16 or wider, within the bound.
A program may use at most 384 MiB of HBM per device.

v0:
```python
import jax
import jax.numpy as jnp
from jax import lax
from jax.sharding import PartitionSpec as P

HEAD_DIM = 128


EPSILON = 1e-05
SPARE_ROUTE = 5


def swapped(value, axis, distance):
    mask = 2**distance
    pairs = [(source, source ^ mask) for source in range(lax.axis_size(axis))]
    return lax.ppermute(value, axis, pairs)


def as_sent(value):

    def short(part):
        return part.astype(jnp.bfloat16) if part.dtype == jnp.float32 else part

    return jax.tree.map(short, value)


def shifted(value, axis, steps):
    count = lax.axis_size(axis)
    leading, last = (max(0, -steps), min(count, count - steps))
    return lax.ppermute(value, axis, [(source, source + steps) for source in range(leading, last)])


def rotary(length, head_size):
    half_dim = head_size // 2
    frequency = 10000.0 ** (-2.0 * jnp.arange(half_dim, dtype=jnp.float32) / head_size)
    angles = jnp.arange(length, dtype=jnp.float32)[:, None] * frequency[None, :]
    cosine = jnp.concatenate([jnp.cos(angles), jnp.cos(angles)], axis=1)[:, None, :]
    sine_tab = jnp.concatenate([jnp.sin(angles), jnp.sin(angles)], axis=1)[:, None, :]
    return (cosine, sine_tab)


def turn_half(values):
    half_dim = values.shape[-1] // 2
    return jnp.concatenate([-values[..., half_dim:], values[..., :half_dim]], axis=-1)


def unturn_half(values):
    half_dim = values.shape[-1] // 2
    return jnp.concatenate([values[..., half_dim:], -values[..., :half_dim]], axis=-1)


def rotate(values, cosine, sine_tab):
    return values * cosine + turn_half(values) * sine_tab


def rotate_back(gradient, cosine, sine_tab):
    return gradient * cosine + unturn_half(gradient * sine_tab)


def normalize(values, gain_row):
    factor = lax.rsqrt(jnp.mean(values * values, axis=-1, keepdims=True) + EPSILON)
    scaled = values * factor
    return (scaled, factor, scaled * gain_row)


def normalize_back(gradient, scaled, factor, gain_row):
    grad_hat = gradient * gain_row
    inner_mean = jnp.mean(grad_hat * scaled, axis=-1, keepdims=True)
    return (factor * (grad_hat - scaled * inner_mean), jnp.sum(gradient * scaled, axis=0))


def tanh_gelu(values):
    return jax.nn.gelu(values, approximate=True)


def widths(up_local):
    smallest = up_local.shape[1] // 8
    return [smallest * 2**doubling for doubling in range(4)]


def store(buffer, value, clipped, active):
    updated = lax.dynamic_update_index_in_dim(buffer, value.astype(buffer.dtype), clipped, 0)
    return jnp.where(active, updated, buffer)


def pick(buffer, clipped):
    return lax.dynamic_index_in_dim(buffer, clipped, 0, keepdims=False)


def half_rows(whole, row_axis, which):
    size = whole.shape[row_axis] // 2
    return lax.dynamic_slice_in_dim(whole, which * size, size, axis=row_axis)


def join_rows(own_piece, partner_piece, row_axis, parity):
    lower = jnp.where(parity == 1, partner_piece, own_piece)
    upper = jnp.where(parity == 1, own_piece, partner_piece)
    return jnp.concatenate([lower, upper], axis=row_axis)


def project(full_normed, qkv_w, cosine, sine_tab):
    projected = jnp.einsum("ld,tdc->tlc", full_normed, qkv_w, preferred_element_type=jnp.float32)
    head_shape = (full_normed.shape[0], qkv_w.shape[2] // HEAD_DIM, HEAD_DIM)
    queries = rotate(projected[0].reshape(head_shape), cosine, sine_tab).astype(jnp.bfloat16)
    all_keys = rotate(projected[1].reshape(head_shape), cosine, sine_tab).astype(jnp.bfloat16)
    all_values = projected[2].reshape(head_shape).astype(jnp.bfloat16)
    return (queries, all_keys, all_values)


def attend(queries, all_keys, all_values):
    length = queries.shape[0]
    scores = jnp.einsum(
        "qhd,khd->hqk", queries, all_keys, preferred_element_type=jnp.float32
    ) * HEAD_DIM ** (-0.5)
    causal = jnp.arange(length)[:, None] >= jnp.arange(length)[None, :]
    scores = jnp.where(causal[None], scores, -1e30)
    highest = jnp.max(scores, axis=-1, keepdims=True)
    exponent = jnp.exp(scores - highest)
    probabilities = exponent / jnp.sum(exponent, axis=-1, keepdims=True)
    probs_low = probabilities.astype(jnp.bfloat16)
    mixture = jnp.einsum("hqk,khd->qhd", probs_low, all_values, preferred_element_type=jnp.float32)
    return (probabilities, probs_low, mixture.reshape(length, -1).astype(jnp.bfloat16))


def attn_forward(full_normed, qkv_w, out_w, cosine, sine_tab):
    queries, all_keys, all_values = project(full_normed, qkv_w, cosine, sine_tab)
    _, _, mixture = attend(queries, all_keys, all_values)
    return jnp.einsum("lc,dc->ld", mixture, out_w, preferred_element_type=jnp.float32)


def attn_backward(full_normed, full_grad, qkv_w, out_w, cosine, sine_tab):
    queries, all_keys, all_values = project(full_normed, qkv_w, cosine, sine_tab)
    probabilities, probs_low, mixture = attend(queries, all_keys, all_values)
    length = full_normed.shape[0]
    grad_out_w = jnp.einsum("ld,lc->dc", full_grad, mixture, preferred_element_type=jnp.float32)
    grad_mixture = jnp.einsum("ld,dc->lc", full_grad, out_w, preferred_element_type=jnp.float32)
    grad_mixture = grad_mixture.astype(jnp.bfloat16).reshape(queries.shape)
    grad_probs = jnp.einsum(
        "qhd,khd->hqk", grad_mixture, all_values, preferred_element_type=jnp.float32
    )
    grad_values = jnp.einsum(
        "hqk,qhd->khd", probs_low, grad_mixture, preferred_element_type=jnp.float32
    )
    row_total = jnp.sum(probabilities * grad_probs, axis=-1, keepdims=True)
    grad_scores = (probabilities * (grad_probs - row_total)).astype(jnp.bfloat16)
    scale = HEAD_DIM ** (-0.5)
    grad_queries = (
        jnp.einsum("hqk,khd->qhd", grad_scores, all_keys, preferred_element_type=jnp.float32)
        * scale
    )
    grad_keys = (
        jnp.einsum("hqk,qhd->khd", grad_scores, queries, preferred_element_type=jnp.float32) * scale
    )
    grad_projected = jnp.stack(
        [
            rotate_back(grad_queries, cosine, sine_tab).reshape(length, -1),
            rotate_back(grad_keys, cosine, sine_tab).reshape(length, -1),
            grad_values.reshape(length, -1),
        ]
    ).astype(jnp.bfloat16)
    grad_qkv_w = jnp.einsum(
        "ld,tlc->tdc", full_normed, grad_projected, preferred_element_type=jnp.float32
    )
    grad_normed = jnp.einsum(
        "tlc,tdc->ld", grad_projected, qkv_w, preferred_element_type=jnp.float32
    )
    return (grad_qkv_w, grad_out_w, grad_normed)


def ffn_forward_cols(full_normed, up_w, down_w, columns):

    def run_columns():
        hidden = jnp.dot(full_normed, up_w[:, :columns], preferred_element_type=jnp.float32)
        activation = tanh_gelu(hidden).astype(jnp.bfloat16)
        return jnp.einsum(
            "lf,df->ld", activation, down_w[:, :columns], preferred_element_type=jnp.float32
        )

    return run_columns


def ffn_backward_cols(full_normed, full_grad, up_w, down_w, columns):

    def run_columns(grad_up, grad_down):
        hidden = jnp.dot(full_normed, up_w[:, :columns], preferred_element_type=jnp.float32)
        gelu_out, pullback = jax.vjp(tanh_gelu, hidden)
        activation = gelu_out.astype(jnp.bfloat16)
        grad_act = jnp.einsum(
            "ld,df->lf", full_grad, down_w[:, :columns], preferred_element_type=jnp.float32
        )
        grad_hidden = pullback(grad_act)[0].astype(jnp.bfloat16)
        grad_down = grad_down.at[:, :columns].add(
            jnp.einsum("ld,lf->df", full_grad, activation, preferred_element_type=jnp.float32)
        )
        grad_up = grad_up.at[:, :columns].add(
            jnp.einsum("ld,lf->df", full_normed, grad_hidden, preferred_element_type=jnp.float32)
        )
        grad_normed = jnp.einsum(
            "lf,df->ld", grad_hidden, up_w[:, :columns], preferred_element_type=jnp.float32
        )
        return (grad_up, grad_down, grad_normed)

    return run_columns


def forward_branches(full_normed, weights, cosine, sine_tab, zero_rows):
    qkv_full, out_full, up_full, down_full = weights

    def forward_attention_branch():
        return attn_forward(full_normed, qkv_full, out_full, cosine, sine_tab)

    branches = [forward_attention_branch]
    branches += [
        ffn_forward_cols(full_normed, up_full, down_full, columns) for columns in widths(up_full)
    ]
    branches.append(lambda: zero_rows)
    return branches


def backward_branches(full_normed, full_grad, weights, cosine, sine_tab, zero_rows):
    qkv_full, out_full, up_full, down_full = weights

    def backward_attention_branch(totals):
        step_qkv, step_out, grad_normed = attn_backward(
            full_normed, full_grad, qkv_full, out_full, cosine, sine_tab
        )
        return ((totals[0] + step_qkv, totals[1] + step_out, totals[2], totals[3]), grad_normed)

    def ffn_branch(columns):
        run_columns = ffn_backward_cols(full_normed, full_grad, up_full, down_full, columns)

        def apply_columns(totals):
            grad_up, grad_down, grad_normed = run_columns(totals[2], totals[3])
            return ((totals[0], totals[1], grad_up, grad_down), grad_normed)

        return apply_columns

    def spare_branch(totals):
        return (totals, zero_rows)

    return (
        [backward_attention_branch]
        + [ffn_branch(columns) for columns in widths(up_full)]
        + [spare_branch]
    )


def route_of(active, parity, width_index, clipped):
    width_route = jnp.where(parity == 1, 1 + pick(width_index, clipped), 0)
    return jnp.where(active, width_route, SPARE_ROUTE)


def local(
    inputs,
    cotangent,
    width_index,
    qkv_weight,
    out_weight,
    attn_gain,
    ffn_gain,
    up_weight,
    down_weight,
):
    section_id = lax.axis_index("section")
    section_count = lax.axis_size("section")
    parity = section_id % 2
    partner = swapped(
        (qkv_weight, out_weight, attn_gain, ffn_gain, up_weight, down_weight), "section", 0
    )
    own_half = (qkv_weight, out_weight, attn_gain, ffn_gain, up_weight, down_weight)
    row_axes = (1, 0, 0, 0, 0, 0)
    whole_layer = [
        join_rows(own_piece, partner_piece, row_axis, parity)
        for own_piece, partner_piece, row_axis in zip(own_half, partner, row_axes)
    ]
    qkv_full, out_full, gain_attn, gain_ffn, up_full, down_full = whole_layer
    gain_row = jnp.where(parity == 1, gain_ffn, gain_attn).astype(jnp.float32)
    weights = (qkv_full, out_full, up_full, down_full)
    micro_count, local_len, model_width = inputs.shape
    full_len = local_len * lax.axis_size("mp")
    cosine, sine_tab = rotary(full_len, HEAD_DIM)
    moments = micro_count + section_count - 1
    zero_rows = jnp.zeros((full_len, model_width), jnp.float32)
    layer_out = jnp.zeros_like(inputs)
    kept_in = jnp.zeros_like(inputs)
    incoming = jnp.zeros((local_len, model_width), jnp.bfloat16)
    for moment in range(moments):
        serial = moment - section_id
        active = (serial >= 0) & (serial < micro_count)
        clipped = jnp.clip(serial, 0, micro_count - 1)
        section_in = jnp.where(section_id == 0, pick(inputs, clipped), incoming)
        residual = section_in.astype(jnp.float32)
        _, _, normed = normalize(residual, gain_row)
        full_normed = lax.all_gather(normed.astype(jnp.bfloat16), "mp", axis=0, tiled=True)
        route = route_of(active, parity, width_index, clipped)
        partial_sum = lax.switch(
            route, forward_branches(full_normed, weights, cosine, sine_tab, zero_rows)
        )
        branch = jax.tree.map(
            lambda part: part.astype(jnp.float32),
            lax.psum_scatter(as_sent(partial_sum), "mp", scatter_dimension=0, tiled=True),
        )
        section_out = (residual + branch).astype(jnp.bfloat16)
        layer_out = store(layer_out, section_out, clipped, active)
        kept_in = store(kept_in, section_in, clipped, active)
        if moment + 1 < moments:
            incoming = shifted(section_out, "section", 1)
    totals = (
        jnp.zeros(qkv_full.shape, jnp.float32),
        jnp.zeros(out_full.shape, jnp.float32),
        jnp.zeros(up_full.shape, jnp.float32),
        jnp.zeros(down_full.shape, jnp.float32),
    )
    gain_total = jnp.zeros((model_width,), jnp.float32)
    input_grad = jnp.zeros(inputs.shape, jnp.float32)
    incoming_grad = jnp.zeros((local_len, model_width), jnp.float32)
    for moment in range(moments):
        serial = moment - (section_count - 1 - section_id)
        active = (serial >= 0) & (serial < micro_count)
        clipped = jnp.clip(serial, 0, micro_count - 1)
        own_grad = pick(cotangent, clipped).astype(jnp.float32)
        upstream = jnp.where(section_id == section_count - 1, own_grad, incoming_grad)
        section_in = pick(kept_in, clipped).astype(jnp.float32)
        scaled, factor, normed = normalize(section_in, gain_row)
        full_normed, grad_full = (
            lax.all_gather(normed.astype(jnp.bfloat16), "mp", axis=0, tiled=True),
            lax.all_gather(upstream.astype(jnp.bfloat16), "mp", axis=0, tiled=True),
        )
        route = route_of(active, parity, width_index, clipped)
        totals, grad_normed = lax.switch(
            route,
            backward_branches(full_normed, grad_full, weights, cosine, sine_tab, zero_rows),
            totals,
        )
        grad_normed = jax.tree.map(
            lambda part: part.astype(jnp.float32),
            lax.psum_scatter(as_sent(grad_normed), "mp", scatter_dimension=0, tiled=True),
        )
        grad_hat, gain_term = normalize_back(grad_normed, scaled, factor, gain_row)
        gain_total = gain_total + jnp.where(active, gain_term, jnp.zeros_like(gain_term))
        grad_input = upstream + grad_hat
        input_grad = store(input_grad, grad_input, clipped, active)
        if moment + 1 < moments:
            incoming_grad = shifted(as_sent(grad_input), "section", -1).astype(grad_input.dtype)
    attn_gain_total = jnp.where(parity == 1, jnp.zeros_like(gain_total), gain_total)
    ffn_gain_total = jnp.where(parity == 1, gain_total, jnp.zeros_like(gain_total))
    everything = totals + (attn_gain_total, ffn_gain_total)
    total_axes = (1, 0, 0, 0, 0, 0)
    own_rows = [
        half_rows(whole, row_axis, parity) for whole, row_axis in zip(everything, total_axes)
    ]
    other_rows = [
        half_rows(whole, row_axis, 1 - parity) for whole, row_axis in zip(everything, total_axes)
    ]
    received = swapped(
        (
            as_sent(other_rows[0]),
            as_sent(other_rows[1]),
            as_sent(other_rows[2]),
            as_sent(other_rows[3]),
            as_sent(other_rows[4]),
            as_sent(other_rows[5]),
        ),
        "section",
        0,
    )
    owned = [own_piece + partner_piece for own_piece, partner_piece in zip(own_rows, received)]
    qkv_done, out_done, up_done, down_done = (
        lax.psum_scatter(
            owned[0].astype(jnp.bfloat16), "dp", scatter_dimension=1, tiled=True
        ).astype(jnp.float32),
        lax.psum_scatter(
            owned[1].astype(jnp.bfloat16), "dp", scatter_dimension=0, tiled=True
        ).astype(jnp.float32),
        lax.psum_scatter(
            owned[2].astype(jnp.bfloat16), "dp", scatter_dimension=0, tiled=True
        ).astype(jnp.float32),
        lax.psum_scatter(
            owned[3].astype(jnp.bfloat16), "dp", scatter_dimension=0, tiled=True
        ).astype(jnp.float32),
    )
    attn_gain_done, ffn_gain_done = (
        lax.psum_scatter(owned[4], ("dp", "mp"), scatter_dimension=0, tiled=True),
        lax.psum_scatter(owned[5], ("dp", "mp"), scatter_dimension=0, tiled=True),
    )
    return (
        layer_out[None],
        input_grad.astype(jnp.bfloat16)[None],
        qkv_done,
        out_done,
        attn_gain_done,
        ffn_gain_done,
        up_done,
        down_done,
    )


def solution(mesh):
    in_specs = (
        P("dp", "mp", None),
        P("dp", "mp", None),
        P("dp"),
        P(None, "section", "mp"),
        P("section", "mp"),
        P("section"),
        P("section"),
        P("section", "mp"),
        P("section", "mp"),
    )
    out_specs = (
        P("section", "dp", "mp", None),
        P("section", "dp", "mp", None),
        P(None, ("section", "dp"), "mp"),
        P(("section", "dp"), "mp"),
        P(("section", "dp", "mp")),
        P(("section", "dp", "mp")),
        P(("section", "dp"), "mp"),
        P(("section", "dp"), "mp"),
    )
    return jax.shard_map(local, mesh=mesh, in_specs=in_specs, out_specs=out_specs, check_vma=False)
```

profile of v0, /device:TPU:0, one launch (start us, length us, event | category | flops | bytes accessed | tf_op | source)
XLA Modules:
  0.0 1761.5 jit_solution(6719916753627818911)
XLA Ops:
  18.3 271.1 %collective-permute-done.2 = bf16[768]{0:T(1024)(128)(2,1)S(1)} collective-permute-done((bf16[768]{0:T(1024)(128)(2,1)}, bf16[768]{0:T(1024)(128)(2,1)S(1)}, u32[]{:S(2)}, u32[]{:S(2)}) %collective-permute-start.2) | collective-permute-done | bytes 1568 | tf_op jit(solution)/shard_map/ppermute | solution.py:16
  296.0 20.7 %collective-permute-done.3 = bf16[768,768]{1,0:T(8,128)(2,1)S(1)} collective-permute-done((bf16[768,768]{1,0:T(8,128)(2,1)}, bf16[768,768]{1,0:T(8,128)(2,1)S(1)}, u32[]{:S(2)}, u32[]{:S(2)}) %collective-permute-start.3) | collective-permute-done | bytes 1179680 | tf_op jit(solution)/shard_map/ppermute | solution.py:16
  344.8 24.1 %conditional.10 = (bf16[256,1536]{1,0:T(8,128)(2,1)S(1)}) conditional(s32[]{:T(128)} %clamp.30, (bf16[3,1536,768]{2,1,0:T(8,128)(2,1)}, bf16[256,1536]{1,0:T(8,128)(2,1)S(1)}, f32[256,1,128]{0,2,1:T(8,128)S(1)}, f32[256,1,128]{0,2,1:T(8,128)S(1)}, bf16[1536,768]{1,0:T(8,128)(2,1)}) %tuple.408, ...), branch_computations={%region_1.4_spmd, %region_4.5_spmd, %region_5.6_spmd, %region_6.7_... | conditional | flops 4838916096 | bytes 40644700 | solution.py:296
  394.2 26.2 %conditional.11 = (bf16[256,1536]{1,0:T(8,128)(2,1)S(1)}) conditional(s32[]{:T(128)} %clamp.31, (bf16[3,1536,768]{2,1,0:T(8,128)(2,1)}, bf16[256,1536]{1,0:T(8,128)(2,1)S(1)}, f32[256,1,128]{0,2,1:T(8,128)S(1)}, f32[256,1,128]{0,2,1:T(8,128)S(1)}, bf16[1536,768]{1,0:T(8,128)(2,1)}) %tuple.412, ...), branch_computations={%region_11.14_spmd, %region_14.15_spmd, %region_15.16_spmd, %regio... | conditional | flops 4838916096 | bytes 40644700 | solution.py:296
  434.4 8.2 collective-permute-done.7
  455.2 28.5 %reduce-scatter.19.cloned.1.call-done = bf16[128,1536]{1,0:T(8,128)(2,1)} async-done(((bf16[256,1536]{1,0:T(8,128)(2,1)}), bf16[128,1536]{1,0:T(8,128)(2,1)}) %reduce-scatter.19.cloned.1.call-update) | async-done | bytes 393232 | tf_op jit(solution)/shard_map/reduce_scatter | solution.py:301
  489.4 8.1 collective-permute-done.8
  501.4 10.3 conditional.13
  512.6 32.0 %reduce-scatter.21.cloned.1.call-done = bf16[128,1536]{1,0:T(8,128)(2,1)} async-done(((bf16[256,1536]{1,0:T(8,128)(2,1)}), bf16[128,1536]{1,0:T(8,128)(2,1)}) %reduce-scatter.21.cloned.1.call-update) | async-done | bytes 393232 | tf_op jit(solution)/shard_map/reduce_scatter | solution.py:301
  562.3 48.0 %conditional.15 = (f32[3,1536,768]{1,2,0:T(8,128)}, f32[1536,768]{0,1:T(8,128)}, f32[1536,3072]{1,0:T(8,128)}, f32[1536,3072]{1,0:T(8,128)}, bf16[256,1536]{1,0:T(8,128)(2,1)S(1)}) conditional(s32[]{:T(128)} %clamp.35, (bf16[3,1536,768]{2,1,0:T(8,128)(2,1)}, bf16[256,1536]{1,0:T(8,128)(2,1)S(1)}, ...), branch_computations={%region_51.55_spmd, %region_55.57_spmd, %region_57.59_spmd, %regio... | conditional | flops 12102402048 | bytes 225706080 | solution.py:330
  592.4 8.8 broadcast.1563.clone
  601.1 8.7 broadcast.1563
  611.2 66.5 %reduce-scatter.25.cloned.1.call-done = bf16[128,1536]{1,0:T(8,128)(2,1)} async-done(((bf16[256,1536]{1,0:T(8,128)(2,1)}), bf16[128,1536]{1,0:T(8,128)(2,1)}) %reduce-scatter.25.cloned.1.call-update) | async-done | bytes 393232 | tf_op jit(solution)/shard_map/reduce_scatter | solution.py:337
  686.7 8.7 collective-permute-done.10
  697.9 25.3 %conditional.16 = (f32[3,1536,768]{1,2,0:T(8,128)}, f32[1536,768]{0,1:T(8,128)}, f32[1536,3072]{1,0:T(8,128)}, f32[1536,3072]{1,0:T(8,128)}, bf16[256,1536]{1,0:T(8,128)(2,1)}) conditional(s32[]{:T(128)} %clamp.36, (bf16[3,1536,768]{2,1,0:T(8,128)(2,1)}, bf16[256,1536]{1,0:T(8,128)(2,1)S(1)}, ...), branch_computations={%region_66.70_spmd, %region_70.72_spmd, %region_72.74_spmd, %regio... | conditional | flops 12111839232 | bytes 320077920 | solution.py:330
  723.9 123.9 %reduce-scatter.27.cloned.1.call-done = bf16[128,1536]{1,0:T(8,128)(2,1)} async-done(((bf16[256,1536]{1,0:T(8,128)(2,1)}), bf16[128,1536]{1,0:T(8,128)(2,1)}) %reduce-scatter.27.cloned.1.call-update) | async-done | bytes 393232 | tf_op jit(solution)/shard_map/reduce_scatter | solution.py:337
  855.7 8.7 collective-permute-done.11
  866.9 25.3 %conditional.17 = (f32[3,1536,768]{1,2,0:T(8,128)}, f32[1536,768]{0,1:T(8,128)}, f32[1536,3072]{1,0:T(8,128)}, f32[1536,3072]{1,0:T(8,128)}, bf16[256,1536]{1,0:T(8,128)(2,1)}) conditional(s32[]{:T(128)} %clamp.37, (bf16[3,1536,768]{2,1,0:T(8,128)(2,1)}, bf16[256,1536]{1,0:T(8,128)(2,1)S(1)}, ...), branch_computations={%region_81.85_spmd, %region_85.87_spmd, %region_87.89_spmd, %regio... | conditional | flops 12111839232 | bytes 320077920 | solution.py:330
  893.0 128.8 %reduce-scatter.29.cloned.1.call-done = bf16[128,1536]{1,0:T(8,128)(2,1)} async-done(((bf16[256,1536]{1,0:T(8,128)(2,1)}), bf16[128,1536]{1,0:T(8,128)(2,1)}) %reduce-scatter.29.cloned.1.call-update) | async-done | bytes 393232 | tf_op jit(solution)/shard_map/reduce_scatter | solution.py:337
  1029.8 8.7 collective-permute-done.12
  1041.0 65.9 %conditional.18 = (f32[3,1536,768]{1,2,0:T(8,128)}, f32[1536,768]{0,1:T(8,128)}, f32[1536,3072]{1,0:T(8,128)}, f32[1536,3072]{1,0:T(8,128)}, bf16[256,1536]{1,0:T(8,128)(2,1)}) conditional(s32[]{:T(128)} %clamp.38, (bf16[3,1536,768]{2,1,0:T(8,128)(2,1)}, bf16[256,1536]{1,0:T(8,128)(2,1)S(1)}, ...), branch_computations={%region_96.100_spmd, %region_100.102_spmd, %region_102.104_spmd, %... | conditional | flops 12111839232 | bytes 386138304 | solution.py:330
  1070.9 12.1 bitcast_add_fusion.8
  1107.7 99.7 %reduce-scatter.31.cloned.1.call-done = bf16[128,1536]{1,0:T(8,128)(2,1)} async-done(((bf16[256,1536]{1,0:T(8,128)(2,1)}), bf16[128,1536]{1,0:T(8,128)(2,1)}) %reduce-scatter.31.cloned.1.call-update) | async-done | bytes 393232 | tf_op jit(solution)/shard_map/reduce_scatter | solution.py:337
  1215.3 8.9 collective-permute-done.13
  1227.3 89.0 %conditional.19 = (f32[1536,3072]{1,0:T(8,128)}, f32[1536,3072]{1,0:T(8,128)}, bf16[256,1536]{1,0:T(8,128)(2,1)}, f32[3,1536,768]{2,1,0:T(8,128)}, f32[1536,768]{1,0:T(8,128)}) conditional(s32[]{:T(128)} %clamp.39, (bf16[3,1536,768]{2,1,0:T(8,128)(2,1)}, bf16[256,1536]{1,0:T(8,128)(2,1)S(1)}, ...), branch_computations={%region_111.115_spmd, %region_115.117_spmd, %region_117.119_spmd, ... | conditional | flops 12111839232 | bytes 364118144 | solution.py:330
  1264.8 12.1 bitcast_add_fusion.12
  1276.9 15.1 copy.620
  1339.7 86.8 %collective-permute-done.15 = bf16[768,768]{1,0:T(8,128)(2,1)S(1)} collective-permute-done((bf16[768,768]{1,0:T(8,128)(2,1)S(1)}, bf16[768,768]{1,0:T(8,128)(2,1)S(1)}, u32[]{:S(2)}, u32[]{:S(2)}) %collective-permute-start.15) | collective-permute-done | bytes 1179680 | tf_op jit(solution)/shard_map/ppermute | solution.py:16
  1441.0 102.7 %collective-permute-done.19 = bf16[768,3072]{1,0:T(8,128)(2,1)S(1)} collective-permute-done((bf16[768,3072]{1,0:T(8,128)(2,1)S(1)}, bf16[768,3072]{1,0:T(8,128)(2,1)S(1)}, u32[]{:S(2)}, u32[]{:S(2)}) %collective-permute-start.19) | collective-permute-done | bytes 4718624 | tf_op jit(solution)/shard_map/ppermute | solution.py:16
  1556.7 101.3 %collective-permute-done.18 = bf16[768,3072]{1,0:T(8,128)(2,1)S(1)} collective-permute-done((bf16[768,3072]{1,0:T(8,128)(2,1)S(1)}, bf16[768,3072]{1,0:T(8,128)(2,1)S(1)}, u32[]{:S(2)}, u32[]{:S(2)}) %collective-permute-start.18) | collective-permute-done | bytes 4718624 | tf_op jit(solution)/shard_map/ppermute | solution.py:16
  1678.0 15.0 all-reduce.8
  1703.4 48.3 %reduce-scatter.39.cloned.1.call-done = bf16[192,3072]{1,0:T(8,128)(2,1)} async-done(((bf16[768,3072]{1,0:T(8,128)(2,1)}), bf16[192,3072]{1,0:T(8,128)(2,1)}) %reduce-scatter.39.cloned.1.call-update) | async-done | bytes 1179664 | tf_op jit(solution)/shard_map/reduce_scatter | solution.py:375
  (438 shorter events, 363.0 us)
Async XLA Ops:
  7.2 370.4 %reduce-scatter.15.cloned.1.call-start = ((), (), s32[]{:S(2)}) async-start(), calls=%async_computation.14 | async-start | bytes 1179648 | tf_op jit(solution)/shard_map/reduce_scatter | solution.py:301
  7.2 322.0 %collective-permute-start.4 = (bf16[768,3072]{1,0:T(8,128)(2,1)}, bf16[768,3072]{1,0:T(8,128)(2,1)}, u32[]{:S(2)}, u32[]{:S(2)}) collective-permute-start(bf16[768,3072]{1,0:T(8,128)(2,1)} %param.176), channel_id=1, source_target_pairs={{0,8},{8,0},{16,24},{24,16},{1,9},{9,1},{17,25},{25,17},{2,10},{10... | collective-permute-start | bytes 14155784 | tf_op jit(solution)/shard_map/ppermute | solution.py:16
  10.2 319.0 %collective-permute-start.5 = (bf16[768,3072]{1,0:T(8,128)(2,1)}, bf16[768,3072]{1,0:T(8,128)(2,1)}, u32[]{:S(2)}, u32[]{:S(2)}) collective-permute-start(bf16[768,3072]{1,0:T(8,128)(2,1)} %param.177), channel_id=1, source_target_pairs={{0,8},{8,0},{16,24},{24,16},{1,9},{9,1},{17,25},{25,17},{2,10},{10... | collective-permute-start | bytes 14155784 | tf_op jit(solution)/shard_map/ppermute | solution.py:16
  10.3 308.1 %collective-permute-start = (bf16[3,768,768]{2,1,0:T(8,128)(2,1)}, bf16[3,768,768]{2,1,0:T(8,128)(2,1)}, u32[]{:S(2)}, u32[]{:S(2)}) collective-permute-start(bf16[3,768,768]{2,1,0:T(8,128)(2,1)} %param.172), channel_id=1, source_target_pairs={{0,8},{8,0},{16,24},{24,16},{1,9},{9,1},{17,25},{25,17},{2,10},{10... | collective-permute-start | bytes 10616840 | tf_op jit(solution)/shard_map/ppermute | solution.py:16
  12.3 277.1 %collective-permute-start.2 = (bf16[768]{0:T(1024)(128)(2,1)}, bf16[768]{0:T(1024)(128)(2,1)S(1)}, u32[]{:S(2)}, u32[]{:S(2)}) collective-permute-start(bf16[768]{0:T(1024)(128)(2,1)} %param.174), channel_id=1, source_target_pairs={{0,8},{8,0},{16,24},{24,16},{1,9},{9,1},{17,25},{25,17},{2,10},{10... | collective-permute-start | bytes 4616 | tf_op jit(solution)/shard_map/ppermute | solution.py:16
  12.3 279.4 %collective-permute-start.1 = (bf16[768]{0:T(1024)(128)(2,1)}, bf16[768]{0:T(1024)(128)(2,1)S(1)}, u32[]{:S(2)}, u32[]{:S(2)}) collective-permute-start(bf16[768]{0:T(1024)(128)(2,1)} %param.175), channel_id=1, source_target_pairs={{0,8},{8,0},{16,24},{24,16},{1,9},{9,1},{17,25},{25,17},{2,10},{10... | collective-permute-start | bytes 4616 | tf_op jit(solution)/shard_map/ppermute | solution.py:16
  289.4 27.4 %collective-permute-start.3 = (bf16[768,768]{1,0:T(8,128)(2,1)}, bf16[768,768]{1,0:T(8,128)(2,1)S(1)}, u32[]{:S(2)}, u32[]{:S(2)}) collective-permute-start(bf16[768,768]{1,0:T(8,128)(2,1)} %param.173), channel_id=1, source_target_pairs={{0,8},{8,0},{16,24},{24,16},{1,9},{9,1},{17,25},{25,17},{2,10},{10... | collective-permute-start | bytes 3538952 | tf_op jit(solution)/shard_map/ppermute | solution.py:16
  369.9 58.9 %reduce-scatter.17.cloned.1.call-start = ((), (), s32[]{:S(2)}) async-start(), calls=%async_computation.15 | async-start | bytes 1179648 | tf_op jit(solution)/shard_map/reduce_scatter | solution.py:301
  378.8 12.5 collective-permute-start.6
  421.3 62.5 %reduce-scatter.19.cloned.1.call-start = ((), (), s32[]{:S(2)}) async-start(), calls=%async_computation.16 | async-start | bytes 1179648 | tf_op jit(solution)/shard_map/reduce_scatter | solution.py:301
  430.1 12.4 collective-permute-start.7
  455.2 89.4 %reduce-scatter.21.cloned.1.call-start = ((), (), s32[]{:S(2)}) async-start(), calls=%async_computation.17 | async-start | bytes 1179648 | tf_op jit(solution)/shard_map/reduce_scatter | solution.py:301
  485.1 12.4 collective-permute-start.8
  511.8 166.0 %reduce-scatter.25.cloned.1.call-start = ((), (), s32[]{:S(2)}) async-start(), calls=%async_computation.19 | async-start | bytes 1179648 | tf_op jit(solution)/shard_map/reduce_scatter | solution.py:337
  545.9 12.7 collective-permute-start.9
  611.2 236.6 %reduce-scatter.27.cloned.1.call-start = ((), (), s32[]{:S(2)}) async-start(), calls=%async_computation.20 | async-start | bytes 1179648 | tf_op jit(solution)/shard_map/reduce_scatter | solution.py:337
  682.2 13.1 collective-permute-start.10
  723.2 298.6 %reduce-scatter.29.cloned.1.call-start = ((), (), s32[]{:S(2)}) async-start(), calls=%async_computation.21 | async-start | bytes 1179648 | tf_op jit(solution)/shard_map/reduce_scatter | solution.py:337
  851.2 13.2 collective-permute-start.11
  892.3 315.1 %reduce-scatter.31.cloned.1.call-start = ((), (), s32[]{:S(2)}) async-start(), calls=%async_computation.22 | async-start | bytes 1179648 | tf_op jit(solution)/shard_map/reduce_scatter | solution.py:337
  1025.3 13.2 collective-permute-start.12
  1107.0 217.1 %reduce-scatter.33.cloned.1.call-start = ((), (), s32[]{:S(2)}) async-start(), calls=%async_computation.23 | async-start | bytes 1179648 | tf_op jit(solution)/shard_map/reduce_scatter | solution.py:337
  1210.9 13.2 collective-permute-start.13
  1316.3 377.8 %reduce-scatter.23.cloned.1.call-start = ((), (), s32[]{:S(2)}) async-start(), calls=%async_computation.18 | async-start | bytes 1179648 | tf_op jit(solution)/shard_map/reduce_scatter | solution.py:301
  1322.4 107.1 %collective-permute-start.14 = (bf16[3,768,768]{2,1,0:T(8,128)(2,1)}, bf16[3,768,768]{2,1,0:T(8,128)(2,1)}, u32[]{:S(2)}, u32[]{:S(2)}) collective-permute-start(bf16[3,768,768]{2,1,0:T(8,128)(2,1)} %dynamic-slice_convert_fusion.2), channel_id=1, source_target_pairs={{0,8},{8,0},{16,24},{24,16},{1,9},{9,1},{17,25},{25,17},{2,10},{10... | collective-permute-start | bytes 10616840 | tf_op jit(solution)/shard_map/ppermute | solution.py:16
  1335.9 360.2 %reduce-scatter.37.cloned.1.call-start = ((), (), s32[]{:S(2)}) async-start(), calls=%async_computation.25 | async-start | bytes 1474560 | tf_op jit(solution)/shard_map/reduce_scatter | solution.py:372
  1337.7 88.7 %collective-permute-start.15 = (bf16[768,768]{1,0:T(8,128)(2,1)S(1)}, bf16[768,768]{1,0:T(8,128)(2,1)S(1)}, u32[]{:S(2)}, u32[]{:S(2)}) collective-permute-start(bf16[768,768]{1,0:T(8,128)(2,1)S(1)} %dynamic-slice_convert_fusion.3), channel_id=1, source_target_pairs={{0,8},{8,0},{16,24},{24,16},{1,9},{9,1},{17,25},{25,17},{2,10},{10... | collective-permute-start | bytes 3538952 | tf_op jit(solution)/shard_map/ppermute | solution.py:16
  1429.4 268.5 %reduce-scatter.35.cloned.1.call-start = ((), (), s32[]{:S(2)}) async-start(), calls=%async_computation.24 | async-start | bytes 4423680 | tf_op jit(solution)/shard_map/reduce_scatter | solution.py:369
  1436.2 264.3 %reduce-scatter.41.cloned.1.call-start = ((), (), s32[]{:S(2)}) async-start(), calls=%async_computation.27 | async-start | bytes 5898240 | tf_op jit(solution)/shard_map/reduce_scatter | solution.py:378
  1440.6 103.1 %collective-permute-start.19 = (bf16[768,3072]{1,0:T(8,128)(2,1)S(1)}, bf16[768,3072]{1,0:T(8,128)(2,1)S(1)}, u32[]{:S(2)}, u32[]{:S(2)}) collective-permute-start(bf16[768,3072]{1,0:T(8,128)(2,1)S(1)} %dynamic-slice_convert_fusion), channel_id=1, source_target_pairs={{0,8},{8,0},{16,24},{24,16},{1,9},{9,1},{17,25},{25,17},{2,10},{10... | collective-permute-start | bytes 14155784 | tf_op jit(solution)/shard_map/ppermute | solution.py:16
  1551.4 200.3 %reduce-scatter.39.cloned.1.call-start = ((), (), s32[]{:S(2)}) async-start(), calls=%async_computation.26 | async-start | bytes 5898240 | tf_op jit(solution)/shard_map/reduce_scatter | solution.py:375
  1555.8 102.2 %collective-permute-start.18 = (bf16[768,3072]{1,0:T(8,128)(2,1)S(1)}, bf16[768,3072]{1,0:T(8,128)(2,1)S(1)}, u32[]{:S(2)}, u32[]{:S(2)}) collective-permute-start(bf16[768,3072]{1,0:T(8,128)(2,1)S(1)} %dynamic-slice_convert_fusion.1), channel_id=1, source_target_pairs={{0,8},{8,0},{16,24},{24,16},{1,9},{9,1},{17,25},{25,17},{2,10},{10... | collective-permute-start | bytes 14155784 | tf_op jit(solution)/shard_map/ppermute | solution.py:16
  (94 other events, 3187.8 us)
Sparse Core Ops, SparseCore 0:
  370.0 7.5 reduce-scatter.14
  421.4 7.3 reduce-scatter.16
  455.3 28.4 reduce-scatter.18
  511.9 32.6 reduce-scatter.20
  611.3 66.3 reduce-scatter.24
  723.3 124.3 reduce-scatter.26
  892.4 129.3 reduce-scatter.28
  1107.1 100.2 reduce-scatter.30
  1316.5 7.5 reduce-scatter.32
  1336.0 14.7 reduce-scatter.22
  1429.5 28.5 reduce-scatter.36
  1460.2 65.0 reduce-scatter.34
  1551.5 84.7 reduce-scatter.40
  1665.8 85.7 reduce-scatter.38
where the time goes:
time: 1750 us; the launch traced here: 1760 us
  waiting for transfers between devices  1200 us (69%)
  loops' own time  158 us (9%)
  other arithmetic  112 us (6%)
  local copies, waits for them, and re-layouts  97.2 us (6%)
  matrix products  91.5 us (5%)
  blocking collectives  50.9 us (3%)
  starting transfers between devices  34.6 us (2%)
  between operations  22.8 us (1%)
    ppermute x12, waiting for transfers between devices, swapped(): return lax.ppermute(value, axis, pairs)  585 us
    reduce_scatter x5, waiting for transfers between devices, local(): lax.psum_scatter(as_sent(grad_normed), 'mp', scatter_dimension=0, tiled=T...  421 us
    another operation x5, loops' own time, local(): lax.switch(route, backward_branches(full_normed, grad_full, weights, cosi...  118 us
    reduce_scatter x5, waiting for transfers between devices, local(): lax.psum_scatter(as_sent(partial_sum), 'mp', scatter_dimension=0, tiled=T...  75.7 us
    ppermute x8, waiting for transfers between devices, shifted(): lax.ppermute(value, axis, [(source, source + steps) for source in range(l...  65.5 us
    reduce_scatter x1, waiting for transfers between devices, local(): lax.psum_scatter(owned[2].astype(jnp.bfloat16), 'dp', scatter_dimension=0...  48.3 us
    another operation x5, loops' own time, local(): lax.switch(route, forward_branches(full_normed, weights, cosine, sine_tab...  39.5 us
  transfers between devices with their start and end apart: 34, of which 25 were waited for; matrix products, arithmetic and copies ran while one was open for 5% of the time, Pallas kernels for 0%

commit v1 on v0

v1 whole, which is shorter than its diff:
```python
import jax
import jax.numpy as jnp
from jax import lax
from jax.sharding import PartitionSpec as P
from jax.experimental import pallas as pl
from jax.experimental.pallas import tpu as pltpu

HEAD_DIM = 128
EPSILON = 1e-05
GELU_C = 0.7978845608028654
GELU_A = 0.044715
MESH = pl.DeviceIdType.MESH
SLOTS = 9
F32 = jnp.float32
BF16 = jnp.bfloat16
VMEM_LIMIT = 60 * 2**20

FWD_RELAYED = ()
BWD_RELAYED = ()


def mm(a, b):
    return lax.dot_general(a, b, (((1,), (0,)), ((), ())), preferred_element_type=F32)


def mm_nt(a, b):
    return lax.dot_general(a, b, (((1,), (1,)), ((), ())), preferred_element_type=F32)


def mm_tn(a, b):
    return lax.dot_general(a, b, (((0,), (0,)), ((), ())), preferred_element_type=F32)


def to_row(column):
    rows = column.shape[0]
    return jnp.transpose(jnp.broadcast_to(column, (rows, 128)))[:8]


def from_row(row):
    return jnp.transpose(row)[:, :1]


def rotary(length, head_size):
    half_dim = head_size // 2
    frequency = 10000.0 ** (-2.0 * jnp.arange(half_dim, dtype=F32) / head_size)
    angles = jnp.arange(length, dtype=F32)[:, None] * frequency[None, :]
    cosine = jnp.concatenate([jnp.cos(angles), jnp.cos(angles)], axis=1)
    sine = jnp.concatenate([-jnp.sin(angles), jnp.sin(angles)], axis=1)
    return cosine, sine


def turned(values):
    return pltpu.roll(values, HEAD_DIM // 2, 1)


def remote(src, dst, send_sem, recv_sem, device):
    return pltpu.make_async_remote_copy(
        src_ref=src, dst_ref=dst, send_sem=send_sem, recv_sem=recv_sem,
        device_id=device, device_id_type=MESH,
    )


class Place:
    def __init__(self):
        section, dp, mp = (lax.axis_index(name) for name in ("section", "dp", "mp"))
        self.block, self.half, self.core = section // 2, section % 2, mp
        other_half = 1 - self.half
        other_block = 1 - self.block
        self.core_peer = (section, dp, 1 - mp)
        self.pair = (self.block * 2 + other_half, dp, mp)
        self.across = (other_block * 2 + self.half, dp, mp)
        self.corner = (other_block * 2 + other_half, dp, mp)

    def barrier(self):
        sem = pltpu.get_barrier_semaphore()
        peers = (self.core_peer, self.pair, self.across, self.corner)
        for peer in peers:
            pl.semaphore_signal(sem, inc=1, device_id=peer, device_id_type=MESH)
        pl.semaphore_wait(sem, len(peers))


class PairLink:
    def __init__(self, place, relayed, relay, send, recv, relay_send, relay_recv, targets):
        self.place, self.relayed, self.relay = place, relayed, relay
        self.send_sem, self.recv_sem = send, recv
        self.relay_send, self.relay_recv = relay_send, relay_recv
        self.targets = targets
        self.started = []

    def start(self, index, src):
        if index in self.relayed:
            at = self.relayed.index(index)
            copy = remote(src, self.relay.at[at], self.send_sem.at[index], self.relay_recv.at[at], self.place.across)
        else:
            copy = remote(src, self.targets(index, self.place.half), self.send_sem.at[index], self.recv_sem.at[index], self.place.pair)
        copy.start()
        self.started.append(copy)

    def wait(self, index):
        dst = self.targets(index, 1 - self.place.half)
        remote(dst, dst, self.send_sem.at[index], self.recv_sem.at[index], self.place.pair).wait_recv()

    def finish(self):
        for copy in self.started:
            copy.wait_send()
        self.started = []

    def forward(self, indices):
        copies = []
        for index in indices:
            if index not in self.relayed:
                continue
            at = self.relayed.index(index)
            held = self.relay.at[at]
            remote(held, held, self.relay_send.at[at], self.relay_recv.at[at], self.place.across).wait_recv()
            copy = remote(held, self.targets(index, self.place.half), self.relay_send.at[at], self.recv_sem.at[index], self.place.corner)
            copy.start()
            copies.append(copy)
        for copy in copies:
            copy.wait_send()


def spread(value, width):
    return jnp.broadcast_to(value, (value.shape[0], width))


def slot_columns(slot, weight, spare, unit):
    if slot in (4, 5):
        return spare[:, (slot - 4) * unit:(slot - 3) * unit]
    at = 0 if slot == 8 else slot * unit
    return weight[:, at:at + unit]


def fill_spare(spare, weight, flag, unit):
    upper = weight[:, 4 * unit:6 * unit].astype(F32)
    lower = weight[:, :2 * unit].astype(F32)
    spare[...] = (upper * flag + lower * (1.0 - flag)).astype(BF16)


def slot_rows(slot, ref, flag):
    if slot in (4, 5):
        mixed = ref[0].astype(F32) * flag + ref[1].astype(F32) * (1.0 - flag)
        return mixed.astype(ref.dtype)
    return ref[1] if slot == 8 else ref[0]


def mask_slot(slot, value, flag):
    return value if slot < 6 else value * flag


def add_slot(slot, totals, value, flag):
    wide, narrow = totals
    if slot in (4, 5):
        return wide + value * flag, narrow + value * (1.0 - flag)
    if slot == 8:
        return wide, narrow + value
    return wide + value, narrow


SLOT_ORDER = (0, 1, 2, 3, 6, 7, 4, 5, 8)


def forward_kernel(
    wide_ref, x0_ref, gain_a_ref, gain_f_ref, cos_ref, sin_ref, wqkv_hbm, wo_hbm, wu_hbm, wd_hbm,
    out_hbm, q_hbm, k_hbm, v_hbm, p_hbm, o_hbm, a_hbm, b_hbm, xa_hbm, xf_hbm, ra_hbm, rf_hbm, u_hbm, g_hbm,
    wqkv, wo, wu, wd, spare_u, spare_d, xa, xf, x2, xg, ab, bb, q, k, v, p, o, ra, rf, u, g,
    own_qkv, snd_qkv, rcv_qkv, snd_u, rcv_u, snd_sq, rcv_sq, snd_br, rcv_br, relay,
    load_sem, x_send, x_recv, relay_send, relay_recv, sq_send, sq_recv, core_send, core_recv,
    in_send, in_recv, in_local, y_send, y_recv, out_send, out_recv, out_local, save_sem,
):
    place = Place()
    half, core = place.half, place.core
    flag = wide_ref[:1, :1]
    seqs, length, feats = xa.shape
    cols = wo.shape[1]
    mine = cols // 2
    heads = mine // HEAD_DIM
    unit = wu.shape[1] // 8
    tokens = length // 2
    full_width = 2 * feats

    loads = [
        pltpu.make_async_copy(src, dst, load_sem.at[n])
        for n, (src, dst) in enumerate(((wqkv_hbm, wqkv), (wo_hbm, wo), (wu_hbm, wu), (wd_hbm, wd)))
    ]
    for load in loads:
        load.start()

    place.barrier()

    def targets(index, sender_half):
        if index < 6:
            return rcv_qkv.at[index // 3, index % 3]
        if index < 8:
            return o.at[index - 6, :, pl.ds(pl.multiple_of(sender_half * mine, mine), mine)]
        return rcv_u.at[index - 8]

    link = PairLink(place, FWD_RELAYED, relay, x_send, x_recv, relay_send, relay_recv, targets)
    every = tuple(range(6 + seqs + SLOTS))
    saves = []

    def save(src, dst):
        copy = pltpu.make_async_copy(src, dst, save_sem.at[len(saves)])
        copy.start()
        saves.append(copy)

    @pl.when(place.block == 1)
    def _():
        link.forward(every)

    my_rows = pl.ds(pl.multiple_of(core * tokens, tokens), tokens)
    my_feats = pl.ds(pl.multiple_of(half * feats, feats), feats)

    def in_copies(i):
        src = x0_ref.at[i, :, my_feats]
        dst = xa.at[i, my_rows, :]
        return (
            pltpu.make_async_copy(src, dst, in_local.at[i]),
            remote(src, dst, in_send.at[i], in_recv.at[i], place.core_peer),
        )

    @pl.when(place.block == 0)
    def _():
        for i in range(seqs):
            for copy in in_copies(i):
                copy.start()

    def wait_input(i):
        @pl.when(place.block == 0)
        def _():
            local, far = in_copies(i)
            local.wait()
            far.wait()

        @pl.when(place.block == 1)
        def _():
            remote(xa.at[i], xa.at[i], y_send.at[i], y_recv.at[i], place.across).wait_recv()

    def sq_copy(n):
        return remote(snd_sq.at[n], rcv_sq.at[n], sq_send.at[n], sq_recv.at[n], place.pair)

    def core_copy(n):
        return remote(snd_br.at[n], rcv_br.at[n], core_send.at[n], core_recv.at[n], place.core_peer)

    def out_piece(i, src_ref):
        return remote(src_ref.at[i, my_rows, :], out_hbm.at[i, :, my_feats], out_send.at[i], out_recv.at[i], place.pair)

    def emit(i, src_ref, owner):
        @pl.when(half == owner)
        def _():
            pltpu.make_async_copy(src_ref.at[i, my_rows, :], out_hbm.at[i, :, my_feats], out_local.at[i]).start()

        @pl.when(half != owner)
        def _():
            out_piece(i, src_ref).start()

    theirs = pl.multiple_of((1 - half) * mine, mine)
    ours = pl.multiple_of(half * mine, mine)
    gain_a = gain_a_ref[...]
    gain_f = gain_f_ref[...]
    for i in range(seqs):
        wait_input(i)
        x = xa[i].astype(F32)
        snd_sq[i] = to_row(jnp.sum(x * x, axis=-1, keepdims=True))
        sq_copy(i).start()
        xg[i] = (x * gain_a).astype(BF16)
        if i == 0:
            loads[0].wait()
        for t in range(3):
            snd_qkv[i, t] = mm(xg[i], wqkv[t, :, pl.ds(theirs, mine)]).astype(BF16)
            link.start(3 * i + t, snd_qkv.at[i, t])
        for t in range(3):
            own_qkv[i, t] = mm(xg[i], wqkv[t, :, pl.ds(ours, mine)])

    cosine, sine = cos_ref[...], sin_ref[...]
    scale = HEAD_DIM ** (-0.5)
    causal = lax.broadcasted_iota(jnp.int32, (length, length), 0) >= lax.broadcasted_iota(jnp.int32, (length, length), 1)
    for i in range(seqs):
        sq_copy(i).wait_recv()
        factor = lax.rsqrt((from_row(snd_sq[i]) + from_row(rcv_sq[i])) * (1.0 / full_width) + EPSILON)
        ra[i] = spread(factor, 128)
        for t in range(3):
            link.wait(3 * i + t)
        for j in range(heads):
            span = pl.ds(j * HEAD_DIM, HEAD_DIM)
            raw = [(own_qkv[i, t, :, span] + rcv_qkv[i, t, :, span].astype(F32)) * factor for t in range(3)]
            q_j = (raw[0] * cosine + turned(raw[0]) * sine).astype(BF16)
            k_j = (raw[1] * cosine + turned(raw[1]) * sine).astype(BF16)
            v_j = raw[2].astype(BF16)
            q[i, :, span], k[i, :, span], v[i, :, span] = q_j, k_j, v_j
            scores = jnp.where(causal, mm_nt(q_j, k_j) * scale, -1e30)
            exponent = jnp.exp(scores - jnp.max(scores, axis=-1, keepdims=True))
            probs = exponent / jnp.sum(exponent, axis=-1, keepdims=True)
            p[i, j] = probs
            o[i, :, pl.ds(pl.multiple_of(ours + j * HEAD_DIM, HEAD_DIM), HEAD_DIM)] = mm(probs.astype(BF16), v_j).astype(BF16)
        link.start(6 + i, o.at[i, :, pl.ds(ours, mine)])
        ab[i] = (xa[i].astype(F32) * factor * gain_a).astype(BF16)

    loads[1].wait()
    for i in range(seqs):
        link.wait(6 + i)
        snd_br[i] = mm_nt(o[i], wo[...]).astype(BF16)
        core_copy(i).start()

    def slot_start(slot):
        part = mm(slot_rows(slot, xg, flag), slot_columns(slot, wu, spare_u, unit))
        u[slot] = part
        snd_u[slot] = part.astype(BF16)
        link.start(8 + slot, snd_u.at[slot])

    loads[2].wait()
    fill_spare(spare_u, wu, flag, unit)
    for i in range(seqs):
        core_copy(i).wait_recv()
        xf[i] = (xa[i].astype(F32) + (snd_br[i].astype(F32) + rcv_br[i].astype(F32))).astype(BF16)
        emit(i, xf, 0)
        x = xf[i].astype(F32)
        snd_sq[2 + i] = to_row(jnp.sum(x * x, axis=-1, keepdims=True))
        sq_copy(2 + i).start()
        xg[i] = (x * gain_f).astype(BF16)
        for slot in SLOT_ORDER[:6] if i == 0 else SLOT_ORDER[6:]:
            slot_start(slot)

    for ref, dst in ((q, q_hbm), (k, k_hbm), (v, v_hbm), (p, p_hbm), (o, o_hbm), (ab, a_hbm), (xa, xa_hbm), (xf, xf_hbm), (ra, ra_hbm)):
        save(ref, dst)

    for i in range(seqs):
        sq_copy(2 + i).wait_recv()
        factor = lax.rsqrt((from_row(snd_sq[2 + i]) + from_row(rcv_sq[2 + i])) * (1.0 / full_width) + EPSILON)
        rf[i] = spread(factor, 128)
        bb[i] = (xf[i].astype(F32) * factor * gain_f).astype(BF16)

    loads[3].wait()
    fill_spare(spare_d, wd, flag, unit)
    totals = (jnp.zeros((length, feats), F32), jnp.zeros((length, feats), F32))
    for slot in SLOT_ORDER:
        link.wait(8 + slot)
        factor = slot_rows(slot, rf, flag)[:, :1]
        z = (u[slot] + rcv_u[slot].astype(F32)) * factor
        u[slot] = z
        active = 0.5 * z * (1.0 + jnp.tanh(GELU_C * (z + GELU_A * (z * z * z))))
        g_k = mask_slot(slot, active, flag).astype(BF16)
        g[slot] = g_k
        totals = add_slot(slot, totals, mm_nt(g_k, slot_columns(slot, wd, spare_d, unit)), flag)
    for i in range(seqs):
        snd_br[2 + i] = totals[i].astype(BF16)
        core_copy(2 + i).start()
    for ref, dst in ((bb, b_hbm), (rf, rf_hbm), (u, u_hbm), (g, g_hbm)):
        save(ref, dst)
    for i in range(seqs):
        core_copy(2 + i).wait_recv()
        x2[i] = (xf[i].astype(F32) + (snd_br[2 + i].astype(F32) + rcv_br[2 + i].astype(F32))).astype(BF16)

        @pl.when(place.block == 0)
        def _():
            remote(x2.at[i], xa.at[i], y_send.at[i], y_recv.at[i], place.across).start()

        emit(i, x2, 1)

    @pl.when(place.block == 0)
    def _():
        link.forward(every)

    link.finish()
    for n in range(4):
        sq_copy(n).wait_send()
        core_copy(n).wait_send()
    for i in range(seqs):
        @pl.when(place.block == 0)
        def _():
            remote(x2.at[i], xa.at[i], y_send.at[i], y_recv.at[i], place.across).wait_send()

        pltpu.make_async_copy(xf.at[i, my_rows, :], out_hbm.at[i, :, my_feats], out_local.at[i]).wait()
        out_piece(i, xf).wait()
    for copy in saves:
        copy.wait()


def backward_kernel(
    wide_ref, c0_ref, gain_a_ref, gain_f_ref, cos_ref, sin_ref, wqkv_hbm, wo_hbm, wu_hbm, wd_hbm,
    q_hbm, k_hbm, v_hbm, p_hbm, xa_hbm, xf_hbm, ra_hbm, rf_hbm, u_hbm,
    ig_hbm, d_hbm, du_hbm, dc_hbm, dqkv_hbm, gain_a_out, gain_f_out,
    wqkv, wo, wu, wd, q, k, v, p, xa, xf, ra, rf, u, spare_u, spare_d,
    e_in, e_bf, e_mid, e, d, dc, du, own_dg, snd_dg, rcv_dg, own_do, snd_do, rcv_do, dqkv,
    snd_row, rcv_row, snd_br, rcv_br, relay,
    load_sem, x_send, x_recv, relay_send, relay_recv, row_send, row_recv, core_send, core_recv,
    in_send, in_recv, in_local, y_send, y_recv, out_send, out_recv, out_local, save_sem,
):
    place = Place()
    half, core = place.half, place.core
    flag = wide_ref[:1, :1]
    seqs, length, feats = xa.shape
    cols = wo.shape[1]
    mine = cols // 2
    heads = mine // HEAD_DIM
    unit = wu.shape[1] // 8
    tokens = length // 2
    full_width = 2 * feats

    sources = (wd_hbm, u_hbm, wu_hbm, xf_hbm, rf_hbm, wo_hbm, q_hbm, k_hbm, v_hbm, p_hbm, wqkv_hbm, xa_hbm, ra_hbm)
    places = (wd, u, wu, xf, rf, wo, q, k, v, p, wqkv, xa, ra)
    loads = [pltpu.make_async_copy(src, dst, load_sem.at[n]) for n, (src, dst) in enumerate(zip(sources, places))]
    for load in loads:
        load.start()

    place.barrier()

    def targets(index, sender_half):
        if index < SLOTS:
            return rcv_dg.at[index]
        if index < SLOTS + seqs:
            return rcv_do.at[index - SLOTS]
        n = index - SLOTS - seqs
        return dqkv.at[n // 3, n % 3, :, pl.ds(pl.multiple_of(sender_half * mine, mine), mine)]

    link = PairLink(place, BWD_RELAYED, relay, x_send, x_recv, relay_send, relay_recv, targets)
    every = tuple(range(SLOTS + seqs + 6))
    saves = []

    def save(src, dst):
        copy = pltpu.make_async_copy(src, dst, save_sem.at[len(saves)])
        copy.start()
        saves.append(copy)

    my_rows = pl.ds(pl.multiple_of(core * tokens, tokens), tokens)
    my_feats = pl.ds(pl.multiple_of(half * feats, feats), feats)

    def in_copies(i):
        src = c0_ref.at[i, :, my_feats]
        dst = e_in.at[i, my_rows, :]
        return (
            pltpu.make_async_copy(src, dst, in_local.at[i]),
            remote(src, dst, in_send.at[i], in_recv.at[i], place.core_peer),
        )

    @pl.when(place.block == 1)
    def _():
        for i in range(seqs):
            for copy in in_copies(i):
                copy.start()

    @pl.when(place.block == 0)
    def _():
        link.forward(every)

    def wait_input(i):
        @pl.when(place.block == 1)
        def _():
            local, far = in_copies(i)
            local.wait()
            far.wait()

        @pl.when(place.block == 0)
        def _():
            remote(e_in.at[i], e_in.at[i], y_send.at[i], y_recv.at[i], place.across).wait_recv()

    def row_copy(n, peer):
        return remote(snd_row.at[n], rcv_row.at[n], row_send.at[n], row_recv.at[n], peer)

    def core_copy(n):
        return remote(snd_br.at[n], rcv_br.at[n], core_send.at[n], core_recv.at[n], place.core_peer)

    def out_piece(i, src_ref):
        return remote(src_ref.at[i, my_rows, :], ig_hbm.at[i, :, my_feats], out_send.at[i], out_recv.at[i], place.pair)

    def emit(i, src_ref, owner):
        @pl.when(half == owner)
        def _():
            pltpu.make_async_copy(src_ref.at[i, my_rows, :], ig_hbm.at[i, :, my_feats], out_local.at[i]).start()

        @pl.when(half != owner)
        def _():
            out_piece(i, src_ref).start()

    theirs = pl.multiple_of((1 - half) * mine, mine)
    ours = pl.multiple_of(half * mine, mine)
    gain_a = gain_a_ref[...]
    gain_f = gain_f_ref[...]

    def norm_back(i, n, x_ref, factor, gain, row_total):
        grad = snd_br[n].astype(F32) + rcv_br[n].astype(F32)
        scaled = x_ref[i].astype(F32) * factor
        mean = row_total * (1.0 / full_width)
        new = e[i] + factor * (grad * gain - scaled * mean)
        return new, jnp.sum(grad * scaled, axis=0, keepdims=True)

    def slot_start(slot):
        part = mm(slot_rows(slot, d, flag), slot_columns(slot, wd, spare_d, unit))
        own_dg[slot] = part
        snd_dg[slot] = part.astype(BF16)
        link.start(slot, snd_dg.at[slot])

    for i in range(seqs):
        wait_input(i)
        e[i] = e_in[i].astype(F32)
        d[i] = e_in[i]
        if i == 0:
            loads[0].wait()
            fill_spare(spare_d, wd, flag, unit)
        for slot in SLOT_ORDER[:6] if i == 0 else SLOT_ORDER[6:]:
            slot_start(slot)
    save(d, d_hbm)

    loads[1].wait()
    loads[2].wait()
    fill_spare(spare_u, wu, flag, unit)
    totals = (jnp.zeros((length, feats), F32), jnp.zeros((length, feats), F32))
    rows = (jnp.zeros((length, 1), F32), jnp.zeros((length, 1), F32))
    for slot in SLOT_ORDER:
        link.wait(slot)
        z = u[slot]
        grad = own_dg[slot] + rcv_dg[slot].astype(F32)
        squared = z * z
        bent = jnp.tanh(GELU_C * (z + GELU_A * (squared * z)))
        slope = 0.5 * (1.0 + bent) + 0.5 * z * (1.0 - bent * bent) * (GELU_C * (1.0 + 3.0 * GELU_A * squared))
        du_k = mask_slot(slot, grad * slope, flag).astype(BF16)
        du[slot] = du_k
        rows = add_slot(slot, rows, jnp.sum(du_k.astype(F32) * z, axis=-1, keepdims=True), flag)
        totals = add_slot(slot, totals, mm_nt(du_k, slot_columns(slot, wu, spare_u, unit)), flag)
    for i in range(seqs):
        snd_br[i] = totals[i].astype(BF16)
        core_copy(i).start()
        snd_row[i] = to_row(rows[i])
        row_copy(i, place.core_peer).start()
    save(du, du_hbm)

    loads[3].wait()
    loads[4].wait()
    loads[5].wait()
    gain_total = jnp.zeros((1, feats), F32)
    for i in range(seqs):
        core_copy(i).wait_recv()
        row_copy(i, place.core_peer).wait_recv()
        new, term = norm_back(i, i, xf, rf[i][:, :1], gain_f, from_row(snd_row[i]) + from_row(rcv_row[i]))
        gain_total = gain_total + term
        e[i] = new
        dc[i] = new.astype(BF16)
        emit(i, dc, 1)
        snd_do[i] = mm(dc[i], wo[:, pl.ds(theirs, mine)]).astype(BF16)
        link.start(SLOTS + i, snd_do.at[i])
        own_do[i] = mm(dc[i], wo[:, pl.ds(ours, mine)])
    gain_f_out[...] = jnp.broadcast_to(gain_total, gain_f_out.shape)
    save(dc, dc_hbm)

    for n in range(6, 10):
        loads[n].wait()
    cosine, sine = cos_ref[...], sin_ref[...]
    scale = HEAD_DIM ** (-0.5)
    for i in range(seqs):
        link.wait(SLOTS + i)
        row = jnp.zeros((length, 1), F32)
        for j in range(heads):
            span = pl.ds(j * HEAD_DIM, HEAD_DIM)
            do_j = (own_do[i, :, span] + rcv_do[i, :, span].astype(F32)).astype(BF16)
            q_j, k_j, v_j, probs = q[i, :, span], k[i, :, span], v[i, :, span], p[i, j]
            dp = mm_nt(do_j, v_j)
            dv = mm_tn(probs.astype(BF16), do_j)
            ds = (probs * (dp - jnp.sum(probs * dp, axis=-1, keepdims=True))).astype(BF16)
            dq = mm(ds, k_j) * scale
            dk = mm_tn(ds, q_j) * scale
            row = row + jnp.sum(dq * q_j.astype(F32) + dk * k_j.astype(F32) + dv * v_j.astype(F32), axis=-1, keepdims=True)
            at = pl.ds(pl.multiple_of(ours + j * HEAD_DIM, HEAD_DIM), HEAD_DIM)
            dqkv[i, 0, :, at] = (dq * cosine - turned(dq) * sine).astype(BF16)
            dqkv[i, 1, :, at] = (dk * cosine - turned(dk) * sine).astype(BF16)
            dqkv[i, 2, :, at] = dv.astype(BF16)
        snd_row[2 + i] = to_row(row)
        row_copy(2 + i, place.pair).start()
        for t in range(3):
            link.start(SLOTS + seqs + 3 * i + t, dqkv.at[i, t, :, pl.ds(ours, mine)])

    for n in range(10, 13):
        loads[n].wait()
    for i in range(seqs):
        part = jnp.zeros((length, feats), F32)
        for t in range(3):
            link.wait(SLOTS + seqs + 3 * i + t)
            part = part + mm_nt(dqkv[i, t], wqkv[t])
        snd_br[2 + i] = part.astype(BF16)
        core_copy(2 + i).start()
        row_copy(2 + i, place.pair).wait_recv()
        snd_row[4 + i] = snd_row[2 + i] + rcv_row[2 + i]
        row_copy(4 + i, place.core_peer).start()
    save(dqkv, dqkv_hbm)

    gain_total = jnp.zeros((1, feats), F32)
    for i in range(seqs):
        core_copy(2 + i).wait_recv()
        row_copy(4 + i, place.core_peer).wait_recv()
        new, term = norm_back(i, 2 + i, xa, ra[i][:, :1], gain_a, from_row(snd_row[4 + i]) + from_row(rcv_row[4 + i]))
        gain_total = gain_total + term
        e_bf[i] = new.astype(BF16)

        @pl.when(place.block == 1)
        def _():
            remote(e_bf.at[i], e_in.at[i], y_send.at[i], y_recv.at[i], place.across).start()

        emit(i, e_bf, 0)
    gain_a_out[...] = jnp.broadcast_to(gain_total, gain_a_out.shape)

    @pl.when(place.block == 1)
    def _():
        link.forward(every)

    link.finish()
    for n in range(6):
        row_copy(n, place.core_peer).wait_send()
    for n in range(4):
        core_copy(n).wait_send()
    for i in range(seqs):
        @pl.when(place.block == 1)
        def _():
            remote(e_bf.at[i], e_in.at[i], y_send.at[i], y_recv.at[i], place.across).wait_send()

        pltpu.make_async_copy(dc.at[i, my_rows, :], ig_hbm.at[i, :, my_feats], out_local.at[i]).wait()
        out_piece(i, dc).wait()
    for copy in saves:
        copy.wait()


def shape(dims, kind):
    return jax.ShapeDtypeStruct(dims, kind)


ANY = pl.BlockSpec(memory_space=pl.ANY)
IN_VMEM = pl.BlockSpec(memory_space=pltpu.VMEM)


def dma(count):
    return pltpu.SemaphoreType.DMA((count,))


def run_forward(wide, x0, gain_a, gain_f, cosine, sine, wqkv, wo, wu, wd):
    seqs, tokens, width = x0.shape
    length, feats, cols, hidden = 2 * tokens, wo.shape[0], wo.shape[1], wu.shape[1]
    mine, unit = cols // 2, hidden // 8
    heads = mine // HEAD_DIM
    out_shape = (
        shape((seqs, tokens, width), BF16),
        shape((seqs, length, mine), BF16),
        shape((seqs, length, mine), BF16),
        shape((seqs, length, mine), BF16),
        shape((seqs, heads, length, length), F32),
        shape((seqs, length, cols), BF16),
        shape((seqs, length, feats), BF16),
        shape((seqs, length, feats), BF16),
        shape((seqs, length, feats), BF16),
        shape((seqs, length, feats), BF16),
        shape((seqs, length, 128), F32),
        shape((seqs, length, 128), F32),
        shape((SLOTS, length, unit), F32),
        shape((SLOTS, length, unit), BF16),
    )
    state = (seqs, length, feats)
    messages = 6 + seqs + SLOTS
    scratch = [
        pltpu.VMEM(wqkv.shape, BF16), pltpu.VMEM(wo.shape, BF16), pltpu.VMEM(wu.shape, BF16), pltpu.VMEM(wd.shape, BF16),
        pltpu.VMEM((feats, 2 * unit), BF16), pltpu.VMEM((feats, 2 * unit), BF16),
        pltpu.VMEM(state, BF16), pltpu.VMEM(state, BF16), pltpu.VMEM(state, BF16), pltpu.VMEM(state, BF16),
        pltpu.VMEM(state, BF16), pltpu.VMEM(state, BF16),
        pltpu.VMEM((seqs, length, mine), BF16), pltpu.VMEM((seqs, length, mine), BF16), pltpu.VMEM((seqs, length, mine), BF16),
        pltpu.VMEM((seqs, heads, length, length), F32),
        pltpu.VMEM((seqs, length, cols), BF16),
        pltpu.VMEM((seqs, length, 128), F32), pltpu.VMEM((seqs, length, 128), F32),
        pltpu.VMEM((SLOTS, length, unit), F32), pltpu.VMEM((SLOTS, length, unit), BF16),
        pltpu.VMEM((seqs, 3, length, mine), F32), pltpu.VMEM((seqs, 3, length, mine), BF16), pltpu.VMEM((seqs, 3, length, mine), BF16),
        pltpu.VMEM((SLOTS, length, unit), BF16), pltpu.VMEM((SLOTS, length, unit), BF16),
        pltpu.VMEM((4, 8, length), F32), pltpu.VMEM((4, 8, length), F32),
        pltpu.VMEM((4, length, feats), BF16), pltpu.VMEM((4, length, feats), BF16),
        pltpu.VMEM((max(len(FWD_RELAYED), 1), length, mine), BF16),
        dma(4), dma(messages), dma(messages), dma(max(len(FWD_RELAYED), 1)), dma(max(len(FWD_RELAYED), 1)),
        dma(4), dma(4), dma(4), dma(4),
        dma(2), dma(2), dma(2), dma(2), dma(2), dma(2), dma(2), dma(2), dma(13),
    ]
    return pl.pallas_call(
        forward_kernel,
        out_shape=out_shape,
        in_specs=[IN_VMEM, ANY, IN_VMEM, IN_VMEM, IN_VMEM, IN_VMEM, ANY, ANY, ANY, ANY],
        out_specs=[ANY] * len(out_shape),
        scratch_shapes=scratch,
        compiler_params=pltpu.CompilerParams(collective_id=1, has_side_effects=True, vmem_limit_bytes=VMEM_LIMIT),
        name="forward",
    )(wide, x0, gain_a, gain_f, cosine, sine, wqkv, wo, wu, wd)


def run_backward(wide, c0, gain_a, gain_f, cosine, sine, wqkv, wo, wu, wd, q, k, v, p, xa, xf, ra, rf, u):
    seqs, tokens, width = c0.shape
    length, feats, cols, hidden = 2 * tokens, wo.shape[0], wo.shape[1], wu.shape[1]
    mine, unit = cols // 2, hidden // 8
    state = (seqs, length, feats)
    out_shape = (
        shape((seqs, tokens, width), BF16),
        shape(state, BF16),
        shape((SLOTS, length, unit), BF16),
        shape(state, BF16),
        shape((seqs, 3, length, cols), BF16),
        shape((8, feats), F32),
        shape((8, feats), F32),
    )
    messages = SLOTS + seqs + 6
    relayed = max(len(BWD_RELAYED), 1)
    scratch = [
        pltpu.VMEM(t.shape, t.dtype) for t in (wqkv, wo, wu, wd, q, k, v, p, xa, xf, ra, rf, u)
    ] + [
        pltpu.VMEM((feats, 2 * unit), BF16), pltpu.VMEM((feats, 2 * unit), BF16),
        pltpu.VMEM(state, BF16), pltpu.VMEM(state, BF16), pltpu.VMEM((1, 8, 128), BF16), pltpu.VMEM(state, F32),
        pltpu.VMEM(state, BF16), pltpu.VMEM(state, BF16),
        pltpu.VMEM((SLOTS, length, unit), BF16),
        pltpu.VMEM((SLOTS, length, unit), F32), pltpu.VMEM((SLOTS, length, unit), BF16), pltpu.VMEM((SLOTS, length, unit), BF16),
        pltpu.VMEM((seqs, length, mine), F32), pltpu.VMEM((seqs, length, mine), BF16), pltpu.VMEM((seqs, length, mine), BF16),
        pltpu.VMEM((seqs, 3, length, cols), BF16),
        pltpu.VMEM((6, 8, length), F32), pltpu.VMEM((6, 8, length), F32),
        pltpu.VMEM((4, length, feats), BF16), pltpu.VMEM((4, length, feats), BF16),
        pltpu.VMEM((relayed, length, mine), BF16),
        dma(13), dma(messages), dma(messages), dma(relayed), dma(relayed), dma(6), dma(6), dma(4), dma(4),
        dma(2), dma(2), dma(2), dma(2), dma(2), dma(2), dma(2), dma(2), dma(4),
    ]
    return pl.pallas_call(
        backward_kernel,
        out_shape=out_shape,
        in_specs=[IN_VMEM, ANY, IN_VMEM, IN_VMEM, IN_VMEM, IN_VMEM] + [ANY] * 13,
        out_specs=[ANY] * 5 + [IN_VMEM] * 2,
        scratch_shapes=scratch,
        compiler_params=pltpu.CompilerParams(collective_id=2, has_side_effects=True, vmem_limit_bytes=VMEM_LIMIT),
        name="backward",
    )(wide, c0, gain_a, gain_f, cosine, sine, wqkv, wo, wu, wd, q, k, v, p, xa, xf, ra, rf, u)


def unpacked(slots, is_wide):
    flag = is_wide > 0
    zero = jnp.zeros_like(slots[0])
    wide_tail = [jnp.where(flag, slots[4], zero), jnp.where(flag, slots[5], zero), slots[6], slots[7]]
    narrow = [jnp.where(flag, slots[8], slots[4]), jnp.where(flag, zero, slots[5])] + [zero] * 6
    wide = [slots[0], slots[1], slots[2], slots[3]] + wide_tail
    return jnp.concatenate([jnp.concatenate(wide, axis=1), jnp.concatenate(narrow, axis=1)], axis=0)


def weight_grad(rows, columns):
    return jnp.einsum("ld,lc->dc", rows, columns, preferred_element_type=F32).astype(BF16)


def local(inputs, cotangent, width_index, qkv_weight, out_weight, attn_gain, ffn_gain, up_weight, down_weight):
    seqs, tokens, width = inputs.shape
    length = 2 * tokens
    swap = width_index[0] < width_index[1]
    is_wide = (jnp.maximum(width_index[0], width_index[1]) == 3).astype(jnp.int32)
    wide = jnp.full((8, 128), is_wide, F32)

    def ordered(value):
        return jnp.where(swap, value[::-1], value)

    cosine, sine = rotary(length, HEAD_DIM)
    gain_a = attn_gain.astype(F32)[None]
    gain_f = ffn_gain.astype(F32)[None]
    weights = (qkv_weight, out_weight, up_weight, down_weight)
    layer_out, q, k, v, p, o, a, b, xa, xf, ra, rf, u, g = run_forward(
        wide, ordered(inputs), gain_a, gain_f, cosine, sine, *weights
    )
    input_grad, d, du, dc, dqkv, gain_a_term, gain_f_term = run_backward(
        wide, ordered(cotangent), gain_a, gain_f, cosine, sine, *weights, q, k, v, p, xa, xf, ra, rf, u
    )
    flat = lambda value: value.reshape(-1, value.shape[-1])
    down_term = weight_grad(flat(d), unpacked(g, is_wide))
    up_term = weight_grad(flat(b), unpacked(du, is_wide))
    out_term = weight_grad(flat(dc), flat(o))
    qkv_term = jnp.einsum("ild,itlc->tdc", a, dqkv, preferred_element_type=F32).astype(BF16)

    def summed(term, axis):
        return lax.psum_scatter(term, "dp", scatter_dimension=axis, tiled=True).astype(F32)

    core = lax.axis_index("mp")

    def gain_grad(term):
        part = lax.psum_scatter(term[0], "dp", scatter_dimension=0, tiled=True)
        size = part.shape[0] // 2
        return lax.dynamic_slice_in_dim(part, core * size, size)

    down_grad = summed(down_term, 0)
    up_grad = summed(up_term, 0)
    out_grad = summed(out_term, 0)
    qkv_grad = summed(qkv_term, 1)
    return (
        ordered(layer_out)[None],
        ordered(input_grad)[None],
        qkv_grad,
        out_grad,
        gain_grad(gain_a_term),
        gain_grad(gain_f_term),
        up_grad,
        down_grad,
    )


def solution(mesh):
    in_specs = (
        P("dp", "mp", None),
        P("dp", "mp", None),
        P("dp"),
        P(None, "section", "mp"),
        P("section", "mp"),
        P("section"),
        P("section"),
        P("section", "mp"),
        P("section", "mp"),
    )
    out_specs = (
        P("section", "dp", "mp", None),
        P("section", "dp", "mp", None),
        P(None, ("section", "dp"), "mp"),
        P(("section", "dp"), "mp"),
        P(("section", "dp", "mp")),
        P(("section", "dp", "mp")),
        P(("section", "dp"), "mp"),
        P(("section", "dp"), "mp"),
    )
    return jax.shard_map(local, mesh=mesh, in_specs=in_specs, out_specs=out_specs, check_vma=False)
```

time: 1750 us -> 725 us (0.41); the launches traced: 1760 us -> 716 us
  waiting for transfers between devices: 1200 us -> 208 us
  Pallas kernels: 0 us -> 410 us
  loops' own time: 158 us -> 0 us
  other arithmetic: 112 us -> 14.7 us
  matrix products: 91.5 us -> 21.8 us
  local copies, waits for them, and re-layouts: 97.2 us -> 28.5 us
  blocking collectives: 50.9 us -> 14.8 us
  starting transfers between devices: 34.6 us -> 0.38 us
    ppermute x20 -> x0, waiting for transfers between devices: 650 us -> none  [the longest x12 585 us: swapped(): return lax.ppermute(value, axis, pairs)]
    pallas_call x0 -> x2, Pallas kernels: none -> 410 us  [the longest x1 300 us: run_backward(): pl.pallas_call(backward_kernel, out_shape=out_shape, in_specs=[IN_VMEM, A...]
    reduce_scatter x14 -> x3, waiting for transfers between devices: 545 us -> 168 us  [summed(): lax.psum_scatter(term, 'dp', scatter_dimension=axis, tiled=True).astype(F32)]
    another operation x10 -> x0, loops' own time: 158 us -> none  [the longest x5 118 us: local(): lax.switch(route, backward_branches(full_normed, grad_full, weights, cosi...]
    dot_general x28 -> x4, matrix products: 85.6 us -> 21.8 us  [the longest x3 17.9 us: weight_grad(): jnp.einsum('ld,lc->dc', rows, columns, preferred_element_type=F32)]
    unnamed x14 -> x5, waiting for transfers between devices: 0.23 us -> 39.7 us
    convert_element_type x27 -> x3, other arithmetic: 46.3 us -> 7.68 us  [summed(): lax.psum_scatter(term, 'dp', scatter_dimension=axis, tiled=True).astype(F32)]
    all_gather x15 -> x0, blocking collectives: 35.9 us -> none  [the longest x10 24.1 us: local(): lax.all_gather(normed.astype(jnp.bfloat16), 'mp', axis=0, tiled=True)]
  transfers between devices with their start and end apart: 34 -> 4, of which waited for: 25 -> 3; matrix products, arithmetic and copies ran while one was open for 5% -> 6% of each run, Pallas kernels for 0% -> 0%
where the time goes in v1:
time: 725 us; the launch traced here: 716 us
  Pallas kernels  410 us (57%)
  waiting for transfers between devices  208 us (29%)
  local copies, waits for them, and re-layouts  28.5 us (4%)
  matrix products  21.8 us (3%)
  between operations  17.7 us (2%)
  blocking collectives  14.8 us (2%)
  other arithmetic  14.7 us (2%)
    pallas_call x1, Pallas kernels, run_backward(): pl.pallas_call(backward_kernel, out_shape=out_shape, in_specs=[IN_VMEM, A...  300 us
    reduce_scatter x3, waiting for transfers between devices, summed(): lax.psum_scatter(term, 'dp', scatter_dimension=axis, tiled=True).astype(F32)  168 us
    pallas_call x1, Pallas kernels, run_forward(): pl.pallas_call(forward_kernel, out_shape=out_shape, in_specs=[IN_VMEM, AN...  110 us
    unnamed x5, waiting for transfers between devices  39.7 us
    unnamed x32, local copies, waits for them, and re-layouts  21.2 us
    dot_general x3, matrix products, weight_grad(): jnp.einsum('ld,lc->dc', rows, columns, preferred_element_type=F32)  17.9 us
    unnamed x1, blocking collectives  14.8 us
  transfers between devices with their start and end apart: 4, of which 3 were waited for; matrix products, arithmetic and copies ran while one was open for 6% of the time, Pallas kernels for 0%

profile of v1, /device:TPU:0, one launch (start us, length us, event | category | flops | bytes accessed | tf_op | source)
XLA Modules:
  0.0 716.0 jit_solution(2466826009873836885)
XLA Ops:
  7.2 1.3 fusion.21
  11.1 1.3 reshape.61.gain_a_ref
  12.4 1.3 reshape.62.gain_f_ref
  14.2 3.4 reverse_select_fusion.1
  17.5 0.8 pad_maximum_fusion.2
  19.0 110.4 %forward.1 = (bf16[2,128,1536]{2,1,0:T(8,128)(2,1)}, bf16[2,256,384]{2,1,0:T(8,128)(2,1)}, bf16[2,256,384]{2,1,0:T(8,128)(2,1)}, bf16[2,256,384]{2,1,0:T(8,128)(...) custom-call(f32[8,128]{1,0:T(8,128)} %broadcast_in_dim.21.wide_ref, ...), custom_call_target="tpu_custom_call" | custom-call | tf_op jit(solution)/shard_map/forward/pallas_call | solution.py:674
  129.4 300.1 %backward.1 = (bf16[2,128,1536]{2,1,0:T(8,128)(2,1)}, bf16[2,256,768]{2,1,0:T(8,128)(2,1)}, bf16[9,256,384]{2,1,0:T(8,128)(2,1)}, bf16[2,256,768]{2,1,0:T(8,128)...) custom-call(f32[8,128]{1,0:T(8,128)} %broadcast_in_dim.21.wide_ref, ...), custom_call_target="tpu_custom_call" | custom-call | tf_op jit(solution)/shard_map/backward/pallas_call | solution.py:717
  429.5 3.0 bitcast_convert_fusion.1
  432.7 3.9 fusion
  436.6 5.7 copy.26
  442.3 4.9 copy.28
  447.3 1.4 copy-done.1
  449.3 0.8 copy-done.5
  450.1 7.5 %convolution_convert_fusion.1 = bf16[768,3072]{1,0:T(8,128)(2,1)} fusion(bf16[512,768]{1,0:T(8,128)(2,1)S(1)} %bitcast.77, bf16[256,2304]{1,0:T(8,128)(2,1)S(1)} %broadcast.34, bf16[256,384]{1,0:T(8,128)(2,1)S(1)} %get-tuple-element.71, bf16[256,384]{1,0:T(8,128)(2,1)S(1)} %get-tuple-element.70, bf16[256,3072]{1,0:T(8,128)(2,1)S(1)} %bitcast_dynamic-update-slice_fusion.8), kind=kOutput, calls=%fused_computation.2 | convolution fusion | flops 2430861312 | bytes 8650752 | tf_op jit(solution)/shard_map/ld,lc->dc/dot_general | solution.py:738
  457.6 1.4 copy-done
  459.5 0.8 copy-done.4
  460.3 7.5 %convolution_convert_fusion = bf16[768,3072]{1,0:T(8,128)(2,1)} fusion(bf16[512,768]{1,0:T(8,128)(2,1)S(1)} %bitcast.76, bf16[256,2304]{1,0:T(8,128)(2,1)S(1)} %broadcast.34, bf16[256,384]{1,0:T(8,128)(2,1)S(1)} %get-tuple-element.69, bf16[256,384]{1,0:T(8,128)(2,1)S(1)} %get-tuple-element.68, bf16[256,3072]{1,0:T(8,128)(2,1)S(1)} %bitcast_dynamic-update-slice_fusion), kind=kOutput, calls=%fused_computation.1 | convolution fusion | flops 2430861312 | bytes 8650752 | tf_op jit(solution)/shard_map/ld,lc->dc/dot_general | solution.py:738
  467.8 0.6 copy-done.7
  469.7 0.8 slice_reduce_fusion.1
  470.5 0.8 slice_reduce_fusion
  471.2 14.8 %all-reduce.2 = (f32[768]{0:T(1024)S(1)}, f32[768]{0:T(1024)S(1)}) all-reduce(f32[768]{0:T(1024)S(1)} %slice_reduce_fusion.1, f32[768]{0:T(1024)S(1)} %slice_reduce_fusion), channel_id=4, replica_groups=mesh['section'=4,'dp'=4,'mp'=2] {'dp'}, use_global_device_ids=true, to_apply=%region_2.3.clone | all-reduce | flops 1536 | bytes 12288
  487.2 1.0 fusion.13
  488.2 1.0 fusion.14
  489.3 1.8 convert_element_type.46
  491.1 39.7 %reduce-scatter.13.cloned.1.call-done = bf16[192,2304]{1,0:T(8,128)(2,1)} async-done(((bf16[768,2304]{1,0:T(8,128)(2,1)}), bf16[192,2304]{1,0:T(8,128)(2,1)}) %reduce-scatter.13.cloned.1.call-update) | async-done | bytes 884752
  530.8 2.2 reshape.67
  532.9 0.9 copy.27
  533.9 1.5 copy.22
  535.4 82.8 %reduce-scatter.9.cloned.1.call-done = bf16[192,3072]{1,0:T(8,128)(2,1)} async-done(((bf16[768,3072]{1,0:T(8,128)(2,1)}), bf16[192,3072]{1,0:T(8,128)(2,1)}) %reduce-scatter.9.cloned.1.call-update) | async-done | bytes 1179664 | tf_op jit(solution)/shard_map/reduce_scatter | solution.py:768
  618.2 2.9 convert_element_type.48
  621.1 85.0 %reduce-scatter.11.cloned.1.call-done = bf16[192,3072]{1,0:T(8,128)(2,1)} async-done(((bf16[768,3072]{1,0:T(8,128)(2,1)}), bf16[192,3072]{1,0:T(8,128)(2,1)}) %reduce-scatter.11.cloned.1.call-update) | async-done | bytes 1179664 | tf_op jit(solution)/shard_map/reduce_scatter | solution.py:768
  706.1 2.9 convert_element_type.50
  (45 shorter events, 4.2 us)
Async XLA Ops:
  7.2 482.1 %reduce-scatter.7.cloned.1.call-start = ((), (), s32[]{:S(2)}) async-start(), calls=%async_computation.4 | async-start | bytes 1474560 | tf_op jit(solution)/shard_map/reduce_scatter | solution.py:768
  129.4 300.1 %copy-start.6 = (bf16[2,256,768]{2,1,0:T(8,128)(2,1)S(1)}, bf16[2,256,768]{2,1,0:T(8,128)(2,1)}, u32[]{:S(2)}) copy-start(bf16[2,256,768]{2,1,0:T(8,128)(2,1)} %get-tuple-element.43) | copy-start | bytes 2359300
  432.5 98.3 %reduce-scatter.13.cloned.1.call-start = ((), (), s32[]{:S(2)}) async-start(), calls=%async_computation.7 | async-start | bytes 4423680
  447.2 1.5 copy-start.1
  447.3 170.9 %reduce-scatter.9.cloned.1.call-start = ((), (), s32[]{:S(2)}) async-start(), calls=%async_computation.5 | async-start | bytes 5898240 | tf_op jit(solution)/shard_map/reduce_scatter | solution.py:768
  448.9 1.1 copy-start.5
  457.5 1.5 copy-start
  457.6 248.6 %reduce-scatter.11.cloned.1.call-start = ((), (), s32[]{:S(2)}) async-start(), calls=%async_computation.6 | async-start | bytes 5898240 | tf_op jit(solution)/shard_map/reduce_scatter | solution.py:768
  459.1 1.1 copy-start.4
  467.8 0.7 copy-start.7
  467.8 19.4 %copy-start.2 = (bf16[2,128,1536]{2,1,0:T(8,128)(2,1)S(1)}, bf16[2,128,1536]{2,1,0:T(8,128)(2,1)}, u32[]{:S(2)}) copy-start(bf16[2,128,1536]{2,1,0:T(8,128)(2,1)} %get-tuple-element.29) | copy-start | bytes 2359300
  467.8 20.4 %copy-start.3 = (bf16[2,128,1536]{2,1,0:T(8,128)(2,1)S(1)}, bf16[2,128,1536]{2,1,0:T(8,128)(2,1)}, u32[]{:S(2)}) copy-start(bf16[2,128,1536]{2,1,0:T(8,128)(2,1)} %get-tuple-element.39) | copy-start | bytes 2359300
Sparse Core Ops, SparseCore 0:
  432.6 30.2 reduce-scatter.6
  465.2 65.5 reduce-scatter.12
  533.1 85.0 reduce-scatter.8
  620.3 85.7 reduce-scatter.10

commit v2 on v1

--- a/solution.py
+++ b/solution.py
@@ -15,8 +15,8 @@
 BF16 = jnp.bfloat16
 VMEM_LIMIT = 60 * 2**20
 
-FWD_RELAYED = ()
-BWD_RELAYED = ()
+FWD_RELAYED = (0, 3, 4, 8, 10, 14, 12)
+BWD_RELAYED = (0, 2, 6, 4, 11, 14, 15)
 
 
 def mm(a, b):
@@ -105,12 +105,9 @@
             copy.wait_send()
         self.started = []
 
-    def forward(self, indices):
+    def forward(self):
         copies = []
-        for index in indices:
-            if index not in self.relayed:
-                continue
-            at = self.relayed.index(index)
+        for at, index in enumerate(self.relayed):
             held = self.relay.at[at]
             remote(held, held, self.relay_send.at[at], self.relay_recv.at[at], self.place.across).wait_recv()
             copy = remote(held, self.targets(index, self.place.half), self.relay_send.at[at], self.recv_sem.at[index], self.place.corner)
@@ -196,7 +193,6 @@
         return rcv_u.at[index - 8]
 
     link = PairLink(place, FWD_RELAYED, relay, x_send, x_recv, relay_send, relay_recv, targets)
-    every = tuple(range(6 + seqs + SLOTS))
     saves = []
 
     def save(src, dst):
@@ -206,7 +202,7 @@
 
     @pl.when(place.block == 1)
     def _():
-        link.forward(every)
+        link.forward()
 
     my_rows = pl.ds(pl.multiple_of(core * tokens, tokens), tokens)
     my_feats = pl.ds(pl.multiple_of(half * feats, feats), feats)
@@ -359,7 +355,7 @@
 
     @pl.when(place.block == 0)
     def _():
-        link.forward(every)
+        link.forward()
 
     link.finish()
     for n in range(4):
@@ -414,7 +410,6 @@
         return dqkv.at[n // 3, n % 3, :, pl.ds(pl.multiple_of(sender_half * mine, mine), mine)]
 
     link = PairLink(place, BWD_RELAYED, relay, x_send, x_recv, relay_send, relay_recv, targets)
-    every = tuple(range(SLOTS + seqs + 6))
     saves = []
 
     def save(src, dst):
@@ -441,7 +436,7 @@
 
     @pl.when(place.block == 0)
     def _():
-        link.forward(every)
+        link.forward()
 
     def wait_input(i):
         @pl.when(place.block == 1)
@@ -599,7 +594,7 @@
 
     @pl.when(place.block == 1)
     def _():
-        link.forward(every)
+        link.forward()
 
     link.finish()
     for n in range(6):

time: 725 us -> 645 us (0.89)
  Pallas kernels: 410 us -> 331 us
    pallas_call x1, Pallas kernels: 300 us -> 192 us  [run_backward(): pl.pallas_call(backward_kernel, out_shape=out_shape, in_specs=[IN_VMEM, A...]
    pallas_call x1, Pallas kernels: 110 us -> 140 us  [run_forward(): pl.pallas_call(forward_kernel, out_shape=out_shape, in_specs=[IN_VMEM, AN...]
  transfers between devices with their start and end apart: 4 -> 4, of which waited for: 3 -> 3; matrix products, arithmetic and copies ran while one was open for 6% -> 7% of each run, Pallas kernels for 0% -> 0%
where the time goes in v2:
time: 645 us; the launch traced here: 635 us
  Pallas kernels  331 us (51%)
  waiting for transfers between devices  208 us (32%)
  local copies, waits for them, and re-layouts  28.3 us (4%)
  matrix products  21.8 us (3%)
  between operations  17.5 us (3%)
  other arithmetic  14.7 us (2%)
  blocking collectives  13.3 us (2%)
    pallas_call x1, Pallas kernels, run_backward(): pl.pallas_call(backward_kernel, out_shape=out_shape, in_specs=[IN_VMEM, A...  192 us
    reduce_scatter x3, waiting for transfers between devices, summed(): lax.psum_scatter(term, 'dp', scatter_dimension=axis, tiled=True).astype(F32)  168 us
    pallas_call x1, Pallas kernels, run_forward(): pl.pallas_call(forward_kernel, out_shape=out_shape, in_specs=[IN_VMEM, AN...  140 us
    unnamed x5, waiting for transfers between devices  40.3 us
    unnamed x32, local copies, waits for them, and re-layouts  21 us
    dot_general x3, matrix products, weight_grad(): jnp.einsum('ld,lc->dc', rows, columns, preferred_element_type=F32)  17.9 us
    unnamed x1, blocking collectives  13.3 us
  transfers between devices with their start and end apart: 4, of which 3 were waited for; matrix products, arithmetic and copies ran while one was open for 7% of the time, Pallas kernels for 0%

profile of v2, /device:TPU:0, one launch (start us, length us, event | category | flops | bytes accessed | tf_op | source)
XLA Modules:
  0.0 635.3 jit_solution(2633265918397192279)
XLA Ops:
  7.2 1.3 fusion.21
  11.1 1.3 reshape.61.gain_a_ref
  12.4 1.3 reshape.62.gain_f_ref
  14.2 3.4 reverse_select_fusion.1
  17.5 0.8 pad_maximum_fusion.2
  19.0 139.6 %forward.1 = (bf16[2,128,1536]{2,1,0:T(8,128)(2,1)}, bf16[2,256,384]{2,1,0:T(8,128)(2,1)}, bf16[2,256,384]{2,1,0:T(8,128)(2,1)}, bf16[2,256,384]{2,1,0:T(8,128)(...) custom-call(f32[8,128]{1,0:T(8,128)} %broadcast_in_dim.21.wide_ref, ...), custom_call_target="tpu_custom_call" | custom-call | tf_op jit(solution)/shard_map/forward/pallas_call | solution.py:669
  158.6 191.5 %backward.1 = (bf16[2,128,1536]{2,1,0:T(8,128)(2,1)}, bf16[2,256,768]{2,1,0:T(8,128)(2,1)}, bf16[9,256,384]{2,1,0:T(8,128)(2,1)}, bf16[2,256,768]{2,1,0:T(8,128)...) custom-call(f32[8,128]{1,0:T(8,128)} %broadcast_in_dim.21.wide_ref, ...), custom_call_target="tpu_custom_call" | custom-call | tf_op jit(solution)/shard_map/backward/pallas_call | solution.py:712
  350.1 3.0 bitcast_convert_fusion.1
  353.2 3.9 fusion
  357.1 5.7 copy.26
  362.8 4.9 copy.28
  368.0 1.2 copy-done.1
  369.7 0.8 copy-done.5
  370.5 7.5 %convolution_convert_fusion.1 = bf16[768,3072]{1,0:T(8,128)(2,1)} fusion(bf16[512,768]{1,0:T(8,128)(2,1)S(1)} %bitcast.77, bf16[256,2304]{1,0:T(8,128)(2,1)S(1)} %broadcast.34, bf16[256,384]{1,0:T(8,128)(2,1)S(1)} %get-tuple-element.71, bf16[256,384]{1,0:T(8,128)(2,1)S(1)} %get-tuple-element.70, bf16[256,3072]{1,0:T(8,128)(2,1)S(1)} %bitcast_dynamic-update-slice_fusion.8), kind=kOutput, calls=%fused_computation.2 | convolution fusion | flops 2430861312 | bytes 8650752 | tf_op jit(solution)/shard_map/ld,lc->dc/dot_general | solution.py:733
  378.1 1.4 copy-done
  379.9 0.8 copy-done.4
  380.7 7.5 %convolution_convert_fusion = bf16[768,3072]{1,0:T(8,128)(2,1)} fusion(bf16[512,768]{1,0:T(8,128)(2,1)S(1)} %bitcast.76, bf16[256,2304]{1,0:T(8,128)(2,1)S(1)} %broadcast.34, bf16[256,384]{1,0:T(8,128)(2,1)S(1)} %get-tuple-element.69, bf16[256,384]{1,0:T(8,128)(2,1)S(1)} %get-tuple-element.68, bf16[256,3072]{1,0:T(8,128)(2,1)S(1)} %bitcast_dynamic-update-slice_fusion), kind=kOutput, calls=%fused_computation.1 | convolution fusion | flops 2430861312 | bytes 8650752 | tf_op jit(solution)/shard_map/ld,lc->dc/dot_general | solution.py:733
  388.3 0.6 copy-done.7
  390.1 0.8 slice_reduce_fusion.1
  390.9 0.8 slice_reduce_fusion
  391.6 13.3 %all-reduce.2 = (f32[768]{0:T(1024)S(1)}, f32[768]{0:T(1024)S(1)}) all-reduce(f32[768]{0:T(1024)S(1)} %slice_reduce_fusion.1, f32[768]{0:T(1024)S(1)} %slice_reduce_fusion), channel_id=4, replica_groups=mesh['section'=4,'dp'=4,'mp'=2] {'dp'}, use_global_device_ids=true, to_apply=%region_2.3.clone | all-reduce | flops 1536 | bytes 12288
  406.1 1.0 fusion.13
  407.1 1.0 fusion.14
  408.1 1.8 convert_element_type.46
  409.9 40.3 %reduce-scatter.13.cloned.1.call-done = bf16[192,2304]{1,0:T(8,128)(2,1)} async-done(((bf16[768,2304]{1,0:T(8,128)(2,1)}), bf16[192,2304]{1,0:T(8,128)(2,1)}) %reduce-scatter.13.cloned.1.call-update) | async-done | bytes 884752
  450.2 2.2 reshape.67
  452.4 0.9 copy.27
  453.3 1.5 copy.22
  454.8 82.8 %reduce-scatter.9.cloned.1.call-done = bf16[192,3072]{1,0:T(8,128)(2,1)} async-done(((bf16[768,3072]{1,0:T(8,128)(2,1)}), bf16[192,3072]{1,0:T(8,128)(2,1)}) %reduce-scatter.9.cloned.1.call-update) | async-done | bytes 1179664 | tf_op jit(solution)/shard_map/reduce_scatter | solution.py:763
  537.6 2.9 convert_element_type.48
  540.6 85.0 %reduce-scatter.11.cloned.1.call-done = bf16[192,3072]{1,0:T(8,128)(2,1)} async-done(((bf16[768,3072]{1,0:T(8,128)(2,1)}), bf16[192,3072]{1,0:T(8,128)(2,1)}) %reduce-scatter.11.cloned.1.call-update) | async-done | bytes 1179664 | tf_op jit(solution)/shard_map/reduce_scatter | solution.py:763
  625.6 2.9 convert_element_type.50
  (45 shorter events, 4.2 us)
Async XLA Ops:
  7.2 400.9 %reduce-scatter.7.cloned.1.call-start = ((), (), s32[]{:S(2)}) async-start(), calls=%async_computation.4 | async-start | bytes 1474560 | tf_op jit(solution)/shard_map/reduce_scatter | solution.py:763
  158.6 191.5 %copy-start.6 = (bf16[2,256,768]{2,1,0:T(8,128)(2,1)S(1)}, bf16[2,256,768]{2,1,0:T(8,128)(2,1)}, u32[]{:S(2)}) copy-start(bf16[2,256,768]{2,1,0:T(8,128)(2,1)} %get-tuple-element.43) | copy-start | bytes 2359300
  353.1 97.0 %reduce-scatter.13.cloned.1.call-start = ((), (), s32[]{:S(2)}) async-start(), calls=%async_computation.7 | async-start | bytes 4423680
  367.7 1.5 copy-start.1
  367.7 169.9 %reduce-scatter.9.cloned.1.call-start = ((), (), s32[]{:S(2)}) async-start(), calls=%async_computation.5 | async-start | bytes 5898240 | tf_op jit(solution)/shard_map/reduce_scatter | solution.py:763
  369.4 1.1 copy-start.5
  378.0 1.5 copy-start
  378.0 247.6 %reduce-scatter.11.cloned.1.call-start = ((), (), s32[]{:S(2)}) async-start(), calls=%async_computation.6 | async-start | bytes 5898240 | tf_op jit(solution)/shard_map/reduce_scatter | solution.py:763
  379.6 1.1 copy-start.4
  388.2 0.7 copy-start.7
  388.2 17.9 %copy-start.2 = (bf16[2,128,1536]{2,1,0:T(8,128)(2,1)S(1)}, bf16[2,128,1536]{2,1,0:T(8,128)(2,1)}, u32[]{:S(2)}) copy-start(bf16[2,128,1536]{2,1,0:T(8,128)(2,1)} %get-tuple-element.29) | copy-start | bytes 2359300
  388.2 18.8 %copy-start.3 = (bf16[2,128,1536]{2,1,0:T(8,128)(2,1)S(1)}, bf16[2,128,1536]{2,1,0:T(8,128)(2,1)}, u32[]{:S(2)}) copy-start(bf16[2,128,1536]{2,1,0:T(8,128)(2,1)} %get-tuple-element.39) | copy-start | bytes 2359300
Sparse Core Ops, SparseCore 0:
  353.3 29.0 reduce-scatter.6
  384.6 65.4 reduce-scatter.12
  452.5 85.0 reduce-scatter.8
  539.8 85.7 reduce-scatter.10
